TPU v7x, 256 devices: a whole 4x4x8 slice. The times are simulated.
256 devices in a mesh: section: 4 (over y), dp: 64 (over z, x, core).
Axes of the slice: x: 4, y: 4, z: 8, core: 2. Of those that a mesh axis runs over, the one named last changes fastest.
Arguments:
- saved_inputs: bfloat16 [4, 4, 8192, 2048], P('section', None, 'dp'), may hold values from -60 to 60, as said below
- out_cotangent: bfloat16 [4, 8192, 2048], P(None, 'dp'), may hold values from -16 to 16
- weights: bfloat16 [4, 2048, 2048], P('section', 'dp'), may hold values from -0.125 to 0.125
- gains: float32 [4, 2048], P('section'), may hold values from 0.5 to 1.5
- row_state: float32 [4, 2048], P('section', 'dp'), may hold values from 655.36 to 32768
- col_state: float32 [4, 2048], P('section'), may hold values from 655.36 to 32768
Outputs:
- input_grads: bfloat16 [4, 4, 8192, 2048], P('section', None, 'dp')
- weight_step: float32 [4, 2048, 2048], P('section', 'dp')
- row_new: float32 [4, 2048], P('section', 'dp')
- col_new: float32 [4, 2048], P('section')
- gain_grad: float32 [4, 2048], P('section')
Inputs may be any that keep to these rules, and one draw needn't show every extreme that they name: `saved_inputs`: each section's inputs vary in scale from token to token and from feature to feature.
All inputs are finite; a program needn't handle non-finite values.
Results may differ from a plain program's by a relative error of at most 0.0059.
Values may be sent and summed in bfloat16 or wider, within the bound.
A program may use at most 128 MiB of HBM per device.

v0:
```python
import jax
import jax.numpy as jnp
from jax import lax
from jax.sharding import PartitionSpec as P

D = 2048


DECAY_RATE = 0.9
SQUARE_EPS = 1e-30
NORM_EPS = 1e-06


def from_behind(block, axis, distance):
    devices = range(lax.axis_size(axis))
    route = [(i - distance, i) for i in devices if i - distance in devices]
    return lax.ppermute(block, axis, route)


def section_back(saved_rows, grad_out, full_weight, gain_row):
    inputs_float = saved_rows.astype(jnp.float32)
    inv_rms = lax.rsqrt(jnp.mean(inputs_float * inputs_float, axis=-1, keepdims=True) + NORM_EPS)
    whitened = inputs_float * inv_rms
    normed = (whitened * gain_row).astype(jnp.bfloat16)
    branch = lax.dot_general(
        grad_out, full_weight, (((1,), (1,)), ((), ())), preferred_element_type=jnp.float32
    )
    gained = branch * gain_row
    input_grad = grad_out.astype(jnp.float32) + inv_rms * (
        gained - whitened * jnp.mean(gained * whitened, axis=-1, keepdims=True)
    )
    return (input_grad.astype(jnp.bfloat16), normed, jnp.sum(branch * whitened, axis=0))


def body(saved_inputs, out_cotangent, weights, gains, row_state, col_state):
    section_count = lax.axis_size("section")
    section_index = lax.axis_index("section")
    micro_count = saved_inputs.shape[1]
    token_rows = saved_inputs.shape[2]
    feature_count = saved_inputs.shape[3]
    full_weight = lax.all_gather(weights, "dp", axis=1, tiled=True)[0]
    gain_row = gains[0]
    total_rows = micro_count * token_rows
    saved_flat = saved_inputs[0].reshape(total_rows, feature_count)
    cotangent_flat = out_cotangent.reshape(total_rows, feature_count)
    pieces = 1

    def pass_back(outgoing):
        return from_behind(outgoing, "section", -1)

    piece_rows = token_rows // pieces
    unit_count = micro_count * pieces

    def tick_step(tick, carry):
        outgoing, grads_flat, outs_flat, normed_flat, gain_sum = carry
        incoming = pass_back(outgoing)
        unit_index = tick - (section_count - 1 - section_index)
        is_valid = jnp.logical_and(unit_index >= 0, unit_index < unit_count)
        row_start = jnp.clip(unit_index, 0, unit_count - 1) * piece_rows
        from_loss = lax.dynamic_slice_in_dim(cotangent_flat, row_start, piece_rows, 0)
        grad_out = jnp.where(section_index == section_count - 1, from_loss, incoming)
        saved_rows = lax.dynamic_slice_in_dim(saved_flat, row_start, piece_rows, 0)

        def active(unused):
            return section_back(saved_rows, grad_out, full_weight, gain_row)

        def resting(unused):
            return (
                jnp.zeros((piece_rows, feature_count), jnp.bfloat16),
                jnp.zeros((piece_rows, feature_count), jnp.bfloat16),
                jnp.zeros((feature_count,), jnp.float32),
            )

        input_grad, normed, gain_part = lax.cond(is_valid, active, resting, 0)

        def store_rows(stored_rows, fresh_rows):
            current = lax.dynamic_slice_in_dim(stored_rows, row_start, piece_rows, 0)
            return lax.dynamic_update_slice_in_dim(
                stored_rows, jnp.where(is_valid, fresh_rows, current), row_start, 0
            )

        return (
            input_grad,
            store_rows(grads_flat, grad_out),
            store_rows(outs_flat, input_grad),
            store_rows(normed_flat, normed),
            gain_sum + gain_part,
        )

    empty_rows = jnp.zeros((total_rows, feature_count), jnp.bfloat16)
    start_carry = (
        jnp.zeros((piece_rows, feature_count), jnp.bfloat16),
        empty_rows,
        empty_rows,
        empty_rows,
        jnp.zeros((feature_count,), jnp.float32),
    )
    finished = lax.fori_loop(0, unit_count + section_count - 1, tick_step, start_carry)
    grads_flat, outs_flat, normed_flat, gain_sum = (
        finished[1],
        finished[2],
        finished[3],
        finished[4],
    )
    whole_term = lax.dot_general(
        normed_flat, grads_flat, (((0,), (0,)), ((), ())), preferred_element_type=jnp.float32
    )
    weight_grad = lax.psum_scatter(whole_term, "dp", scatter_dimension=0, tiled=True)
    squares = weight_grad * weight_grad + SQUARE_EPS
    row_fresh = DECAY_RATE * row_state[0] + (1.0 - DECAY_RATE) * jnp.mean(squares, axis=1)
    column_sum, gain_total, row_total = lax.psum(
        (jnp.sum(squares, axis=0), gain_sum, jnp.sum(row_fresh)), "dp"
    )
    col_fresh = DECAY_RATE * col_state[0] + (1.0 - DECAY_RATE) * column_sum / D
    row_mean = row_total / D
    scaled = weight_grad / jnp.sqrt(row_fresh[:, None] * col_fresh[None, :] / row_mean)
    total_square = lax.psum(jnp.sum(scaled * scaled), "dp")
    clip_factor = jnp.maximum(1.0, jnp.sqrt(total_square / (D * D)))
    input_grads = outs_flat.reshape(1, micro_count, token_rows, feature_count)
    return (
        input_grads,
        (scaled / clip_factor)[None],
        row_fresh[None],
        col_fresh[None],
        gain_total[None],
    )


def solution(mesh):
    placed = (
        P("section", None, "dp", None),
        P(None, "dp", None),
        P("section", "dp", None),
        P("section", None),
        P("section", "dp"),
        P("section", None),
    )
    return jax.shard_map(
        body,
        mesh=mesh,
        in_specs=placed,
        out_specs=(
            P("section", None, "dp", None),
            P("section", "dp", None),
            P("section", "dp"),
            P("section", None),
            P("section", None),
        ),
        check_vma=False,
    )
```

profile of v0, /device:TPU:1, one launch (start us, length us, event | category | flops | bytes accessed | tf_op | source)
XLA Modules:
  0.0 757.2 jit_solution(13274545758768787681)
XLA Ops:
  7.2 0.7 all-gather.2.cloned.1.call-update
  8.0 90.0 %all-gather.2.cloned.1.call-done = bf16[1,2048,2048]{2,1,0:T(8,128)(2,1)} async-done(((bf16[1,32,2048]{2,1,0:T(8,128)(2,1)}), bf16[1,2048,2048]{2,1,0:T(8,128)(2,1)}) %all-gather.2.cloned.1.call-update) | async-done | bytes 8388624 | tf_op jit(solution)/shard_map/all_gather | solution.py:41
  98.0 1.6 broadcast_in_dim.10
  99.6 1.6 broadcast_in_dim.10.clone
  101.2 1.6 broadcast_in_dim.10.clone.1
  102.7 0.9 broadcast.65
  103.6 180.6 %while.24 = (s32[]{:T(128)}, bf16[128,2048]{1,0:T(8,128)(2,1)}, bf16[512,2048]{1,0:T(8,128)(2,1)}, bf16[512,2048]{1,0:T(8,128)(2,1)}, bf16[512,2048]{1,0:T(8,128...) while((s32[]{:T(128)}, bf16[128,2048]{1,0:T(8,128)(2,1)}, ...), condition=%wide.region_6.7_spmd.clone, body=%wide.region_0.6_spmd.clone.sunk | while | flops 1080297600 | bytes 22075788 | solution.py:98
  103.6 1.3 collective-permute-start
  104.9 14.1 %collective-permute-done = bf16[128,2048]{1,0:T(8,128)(2,1)S(1)} collective-permute-done((bf16[128,2048]{1,0:T(8,128)(2,1)}, bf16[128,2048]{1,0:T(8,128)(2,1)S(1)}, u32[]{:S(2)}, u32[]{:S(2)}) %collective-permute-start) | collective-permute-done | bytes 524320 | tf_op jit(solution)/shard_map/while/body/eval_jaxpr/ppermute | solution.py:17
  119.0 2.3 select_dynamic-update-slice_fusion.5
  121.3 1.0 conditional.3
  121.3 0.9 broadcast.59
  122.2 2.6 select_dynamic-update-slice_fusion.6
  124.8 1.3 collective-permute-start
  126.1 13.1 %collective-permute-done = bf16[128,2048]{1,0:T(8,128)(2,1)S(1)} collective-permute-done((bf16[128,2048]{1,0:T(8,128)(2,1)}, bf16[128,2048]{1,0:T(8,128)(2,1)S(1)}, u32[]{:S(2)}, u32[]{:S(2)}) %collective-permute-start) | collective-permute-done | bytes 524320 | tf_op jit(solution)/shard_map/while/body/eval_jaxpr/ppermute | solution.py:17
  139.3 2.3 select_dynamic-update-slice_fusion.5
  141.5 1.0 conditional.3
  141.5 0.9 broadcast.59
  142.5 2.6 select_dynamic-update-slice_fusion.6
  145.1 1.3 collective-permute-start
  146.4 12.2 %collective-permute-done = bf16[128,2048]{1,0:T(8,128)(2,1)S(1)} collective-permute-done((bf16[128,2048]{1,0:T(8,128)(2,1)}, bf16[128,2048]{1,0:T(8,128)(2,1)S(1)}, u32[]{:S(2)}, u32[]{:S(2)}) %collective-permute-start) | collective-permute-done | bytes 524320 | tf_op jit(solution)/shard_map/while/body/eval_jaxpr/ppermute | solution.py:17
  158.6 2.3 select_dynamic-update-slice_fusion.5
  160.8 1.0 conditional.3
  160.8 0.9 broadcast.59
  161.8 2.6 select_dynamic-update-slice_fusion.6
  164.4 1.3 collective-permute-start
  165.7 31.5 %collective-permute-done = bf16[128,2048]{1,0:T(8,128)(2,1)S(1)} collective-permute-done((bf16[128,2048]{1,0:T(8,128)(2,1)}, bf16[128,2048]{1,0:T(8,128)(2,1)S(1)}, u32[]{:S(2)}, u32[]{:S(2)}) %collective-permute-start) | collective-permute-done | bytes 524320 | tf_op jit(solution)/shard_map/while/body/eval_jaxpr/ppermute | solution.py:17
  197.2 2.3 select_dynamic-update-slice_fusion.5
  199.5 8.1 %conditional.3 = (bf16[128,2048]{1,0:T(8,128)(2,1)}, bf16[128,2048]{1,0:T(8,128)(2,1)S(1)}, f32[2048]{0:T(1024)S(1)}) conditional(s32[]{:T(128)} %convert_element_type.56, () %tuple.68, (bf16[128,2048]{1,0:T(8,128)(2,1)S(1)}, bf16[512,2048]{1,0:T(8,128)(2,1)S(1)}, s32[]{:T(128)}, bf16[2048,2048]{1,0:T(8,128)(2,1)}, f32[1,2048]{1,0:T(1,128)S(1)}) %tuple.69), branch_computations={%region_1.1_spmd, %region_2.5_spmd} | conditional | flops 1079244928 | bytes 14184996 | solution.py:74
  199.5 0.3 fusion.11
  199.8 6.4 fusion.10
  206.2 1.4 fusion.9
  207.5 2.7 select_dynamic-update-slice_fusion.6
  210.3 1.3 collective-permute-start
  211.6 11.2 %collective-permute-done = bf16[128,2048]{1,0:T(8,128)(2,1)S(1)} collective-permute-done((bf16[128,2048]{1,0:T(8,128)(2,1)}, bf16[128,2048]{1,0:T(8,128)(2,1)S(1)}, u32[]{:S(2)}, u32[]{:S(2)}) %collective-permute-start) | collective-permute-done | bytes 524320 | tf_op jit(solution)/shard_map/while/body/eval_jaxpr/ppermute | solution.py:17
  222.8 2.3 select_dynamic-update-slice_fusion.5
  225.1 8.1 %conditional.3 = (bf16[128,2048]{1,0:T(8,128)(2,1)}, bf16[128,2048]{1,0:T(8,128)(2,1)S(1)}, f32[2048]{0:T(1024)S(1)}) conditional(s32[]{:T(128)} %convert_element_type.56, () %tuple.68, (bf16[128,2048]{1,0:T(8,128)(2,1)S(1)}, bf16[512,2048]{1,0:T(8,128)(2,1)S(1)}, s32[]{:T(128)}, bf16[2048,2048]{1,0:T(8,128)(2,1)}, f32[1,2048]{1,0:T(1,128)S(1)}) %tuple.69), branch_computations={%region_1.1_spmd, %region_2.5_spmd} | conditional | flops 1079244928 | bytes 14184996 | solution.py:74
  225.3 6.4 fusion.10
  231.8 1.4 fusion.9
  233.1 2.7 select_dynamic-update-slice_fusion.6
  235.9 1.3 collective-permute-start
  237.2 10.3 %collective-permute-done = bf16[128,2048]{1,0:T(8,128)(2,1)S(1)} collective-permute-done((bf16[128,2048]{1,0:T(8,128)(2,1)}, bf16[128,2048]{1,0:T(8,128)(2,1)S(1)}, u32[]{:S(2)}, u32[]{:S(2)}) %collective-permute-start) | collective-permute-done | bytes 524320 | tf_op jit(solution)/shard_map/while/body/eval_jaxpr/ppermute | solution.py:17
  247.5 2.3 select_dynamic-update-slice_fusion.5
  249.8 8.1 %conditional.3 = (bf16[128,2048]{1,0:T(8,128)(2,1)}, bf16[128,2048]{1,0:T(8,128)(2,1)S(1)}, f32[2048]{0:T(1024)S(1)}) conditional(s32[]{:T(128)} %convert_element_type.56, () %tuple.68, (bf16[128,2048]{1,0:T(8,128)(2,1)S(1)}, bf16[512,2048]{1,0:T(8,128)(2,1)S(1)}, s32[]{:T(128)}, bf16[2048,2048]{1,0:T(8,128)(2,1)}, f32[1,2048]{1,0:T(1,128)S(1)}) %tuple.69), branch_computations={%region_1.1_spmd, %region_2.5_spmd} | conditional | flops 1079244928 | bytes 14184996 | solution.py:74
  250.0 6.4 fusion.10
  256.4 1.4 fusion.9
  257.8 2.7 select_dynamic-update-slice_fusion.6
  260.5 1.3 collective-permute-start
  261.8 9.4 %collective-permute-done = bf16[128,2048]{1,0:T(8,128)(2,1)S(1)} collective-permute-done((bf16[128,2048]{1,0:T(8,128)(2,1)}, bf16[128,2048]{1,0:T(8,128)(2,1)S(1)}, u32[]{:S(2)}, u32[]{:S(2)}) %collective-permute-start) | collective-permute-done | bytes 524320 | tf_op jit(solution)/shard_map/while/body/eval_jaxpr/ppermute | solution.py:17
  271.2 2.3 select_dynamic-update-slice_fusion.5
  273.5 8.1 %conditional.3 = (bf16[128,2048]{1,0:T(8,128)(2,1)}, bf16[128,2048]{1,0:T(8,128)(2,1)S(1)}, f32[2048]{0:T(1024)S(1)}) conditional(s32[]{:T(128)} %convert_element_type.56, () %tuple.68, (bf16[128,2048]{1,0:T(8,128)(2,1)S(1)}, bf16[512,2048]{1,0:T(8,128)(2,1)S(1)}, s32[]{:T(128)}, bf16[2048,2048]{1,0:T(8,128)(2,1)}, f32[1,2048]{1,0:T(1,128)S(1)}) %tuple.69), branch_computations={%region_1.1_spmd, %region_2.5_spmd} | conditional | flops 1079244928 | bytes 14184996 | solution.py:74
  273.8 6.4 fusion.10
  280.2 1.4 fusion.9
  281.6 2.7 select_dynamic-update-slice_fusion.6
  284.3 12.5 %fusion.15 = f32[2048,2048]{1,0:T(8,128)} fusion(bf16[512,2048]{1,0:T(8,128)(2,1)} %get-tuple-element.302, bf16[512,2048]{1,0:T(8,128)(2,1)} %get-tuple-element.303), kind=kOutput, calls=%fused_computation.32 | convolution fusion | flops 4294967296 | bytes 20971520 | tf_op jit(solution)/shard_map/dot_general | solution.py:105
  296.8 0.7 copy-done.3
  297.5 184.6 %reduce-scatter.2.cloned.1.call-done = f32[32,2048]{1,0:T(8,128)} async-done(((f32[2048,2048]{1,0:T(8,128)}), f32[32,2048]{1,0:T(8,128)}) %reduce-scatter.2.cloned.1.call-update) | async-done | bytes 262160 | tf_op jit(solution)/shard_map/reduce_scatter | solution.py:108
  482.1 1.1 fusion.12
  483.2 0.6 fusion.14
  483.8 0.5 bitcast_add_fusion
  484.3 132.5 %all-reduce.1 = (f32[]{:T(128)}, f32[2048]{0:T(1024)S(1)}) all-reduce(f32[]{:T(128)} %get-tuple-element.381, f32[2048]{0:T(1024)S(1)} %get-tuple-element.349), channel_id=1, replica_groups=mesh['section'=4,'dp'=64] {'dp'}, use_global_device_ids=true, to_apply=%region_12.13 | all-reduce | flops 2049 | bytes 16392 | tf_op jit(solution)/shard_map/psum | solution.py:111
  617.5 1.7 multiply_reduce_fusion
  619.2 128.7 %all-reduce = (f32[]{:T(128)}, f32[1,2048]{1,0:T(1,128)}) all-reduce(f32[]{:T(128)} %multiply_reduce_fusion, f32[1,2048]{1,0:T(1,128)S(1)} %bitcast.25), channel_id=1, replica_groups=mesh['section'=4,'dp'=64] {'dp'}, use_global_device_ids=true, to_apply=%region_14.15 | all-reduce | flops 2049 | bytes 16392 | tf_op jit(solution)/shard_map/psum | solution.py:117
  748.6 1.8 divide_bitcast_fusion
  (39 shorter events, 1.1 us)
Async XLA Ops:
  7.2 90.8 %all-gather.2.cloned.1.call-start = ((), (), s32[]{:S(2)}) async-start(), calls=%async_computation.1 | async-start | bytes 8519680 | tf_op jit(solution)/shard_map/all_gather | solution.py:41
  7.9 474.2 %reduce-scatter.2.cloned.1.call-start = ((), (), s32[]{:S(2)}) async-start(), calls=%async_computation.2 | async-start | bytes 17039360 | tf_op jit(solution)/shard_map/reduce_scatter | solution.py:108
  99.6 4.0 copy-start
  99.6 4.0 copy-start.1
  103.6 15.4 %collective-permute-start = (bf16[128,2048]{1,0:T(8,128)(2,1)}, bf16[128,2048]{1,0:T(8,128)(2,1)S(1)}, u32[]{:S(2)}, u32[]{:S(2)}) collective-permute-start(bf16[128,2048]{1,0:T(8,128)(2,1)} %get-tuple-element.500), channel_id=1, source_target_pairs={{64,0},{128,64},{192,128},{65,1},{129,65},{193,129},{66,2},{130,66... | collective-permute-start | bytes 1572872 | tf_op jit(solution)/shard_map/while/body/eval_jaxpr/ppermute | solution.py:17
  124.8 14.4 %collective-permute-start = (bf16[128,2048]{1,0:T(8,128)(2,1)}, bf16[128,2048]{1,0:T(8,128)(2,1)S(1)}, u32[]{:S(2)}, u32[]{:S(2)}) collective-permute-start(bf16[128,2048]{1,0:T(8,128)(2,1)} %get-tuple-element.500), channel_id=1, source_target_pairs={{64,0},{128,64},{192,128},{65,1},{129,65},{193,129},{66,2},{130,66... | collective-permute-start | bytes 1572872 | tf_op jit(solution)/shard_map/while/body/eval_jaxpr/ppermute | solution.py:17
  145.1 13.5 %collective-permute-start = (bf16[128,2048]{1,0:T(8,128)(2,1)}, bf16[128,2048]{1,0:T(8,128)(2,1)S(1)}, u32[]{:S(2)}, u32[]{:S(2)}) collective-permute-start(bf16[128,2048]{1,0:T(8,128)(2,1)} %get-tuple-element.500), channel_id=1, source_target_pairs={{64,0},{128,64},{192,128},{65,1},{129,65},{193,129},{66,2},{130,66... | collective-permute-start | bytes 1572872 | tf_op jit(solution)/shard_map/while/body/eval_jaxpr/ppermute | solution.py:17
  164.4 32.8 %collective-permute-start = (bf16[128,2048]{1,0:T(8,128)(2,1)}, bf16[128,2048]{1,0:T(8,128)(2,1)S(1)}, u32[]{:S(2)}, u32[]{:S(2)}) collective-permute-start(bf16[128,2048]{1,0:T(8,128)(2,1)} %get-tuple-element.500), channel_id=1, source_target_pairs={{64,0},{128,64},{192,128},{65,1},{129,65},{193,129},{66,2},{130,66... | collective-permute-start | bytes 1572872 | tf_op jit(solution)/shard_map/while/body/eval_jaxpr/ppermute | solution.py:17
  210.3 12.5 %collective-permute-start = (bf16[128,2048]{1,0:T(8,128)(2,1)}, bf16[128,2048]{1,0:T(8,128)(2,1)S(1)}, u32[]{:S(2)}, u32[]{:S(2)}) collective-permute-start(bf16[128,2048]{1,0:T(8,128)(2,1)} %get-tuple-element.500), channel_id=1, source_target_pairs={{64,0},{128,64},{192,128},{65,1},{129,65},{193,129},{66,2},{130,66... | collective-permute-start | bytes 1572872 | tf_op jit(solution)/shard_map/while/body/eval_jaxpr/ppermute | solution.py:17
  235.9 11.6 %collective-permute-start = (bf16[128,2048]{1,0:T(8,128)(2,1)}, bf16[128,2048]{1,0:T(8,128)(2,1)S(1)}, u32[]{:S(2)}, u32[]{:S(2)}) collective-permute-start(bf16[128,2048]{1,0:T(8,128)(2,1)} %get-tuple-element.500), channel_id=1, source_target_pairs={{64,0},{128,64},{192,128},{65,1},{129,65},{193,129},{66,2},{130,66... | collective-permute-start | bytes 1572872 | tf_op jit(solution)/shard_map/while/body/eval_jaxpr/ppermute | solution.py:17
  260.5 10.7 %collective-permute-start = (bf16[128,2048]{1,0:T(8,128)(2,1)}, bf16[128,2048]{1,0:T(8,128)(2,1)S(1)}, u32[]{:S(2)}, u32[]{:S(2)}) collective-permute-start(bf16[128,2048]{1,0:T(8,128)(2,1)} %get-tuple-element.500), channel_id=1, source_target_pairs={{64,0},{128,64},{192,128},{65,1},{129,65},{193,129},{66,2},{130,66... | collective-permute-start | bytes 1572872 | tf_op jit(solution)/shard_map/while/body/eval_jaxpr/ppermute | solution.py:17
  296.8 0.7 copy-start.3
  296.8 186.4 %copy-start.4 = (f32[1,32]{1,0:T(1,128)S(1)}, f32[1,32]{1,0:T(1,128)}, u32[]{:S(2)}) copy-start(f32[1,32]{1,0:T(1,128)} %param.14) | copy-start | bytes 388
  616.9 133.5 %copy-start.2 = (f32[2048]{0:T(1024)}, f32[2048]{0:T(1024)S(1)}, u32[]{:S(2)}) copy-start(f32[2048]{0:T(1024)S(1)} %multiply_add_fusion.1) | copy-start | bytes 24580
Sparse Core Ops, SparseCore 0:
  10.8 87.1 all-gather.1
  296.9 185.1 reduce-scatter.1
where the time goes:
time: 758 us; the launch traced here: 757 us
  waiting for transfers between devices  377 us (50%)
  blocking collectives  261 us (34%)
  other arithmetic  46.7 us (6%)
  matrix products  38.2 us (5%)
  between operations  15.4 us (2%)
  local copies, waits for them, and re-layouts  9.14 us (1%)
  starting transfers between devices  9.04 us (1%)
    reduce_scatter x1, waiting for transfers between devices, body(): lax.psum_scatter(whole_term, 'dp', scatter_dimension=0, tiled=True)  185 us
    psum x1, blocking collectives, body(): lax.psum((jnp.sum(squares, axis=0), gain_sum, jnp.sum(row_fresh)), 'dp')  133 us
    psum x1, blocking collectives, body(): total_square = lax.psum(jnp.sum(scaled * scaled), 'dp')  129 us
    ppermute x7, waiting for transfers between devices, from_behind(): return lax.ppermute(block, axis, route)  102 us
    all_gather x1, waiting for transfers between devices, body(): full_weight = lax.all_gather(weights, 'dp', axis=1, tiled=True)[0]  90 us
    dynamic_update_slice x14, other arithmetic, store_rows(): lax.dynamic_update_slice_in_dim(stored_rows, jnp.where(is_valid, fresh_ro...  34.4 us
    dot_general x4, matrix products, section_back(): lax.dot_general(grad_out, full_weight, (((1,), (1,)), ((), ())), preferre...  25.7 us
  transfers between devices with their start and end apart: 9, of which 9 were waited for; matrix products, arithmetic and copies ran while one was open for 0% of the time, Pallas kernels for 0%

commit v1 on v0

v1 whole, which is shorter than its diff:
```python
import functools

import jax
import jax.numpy as jnp
from jax import lax
from jax.experimental import pallas as pl
from jax.experimental.pallas import tpu as pltpu
from jax.sharding import PartitionSpec as P

DECAY_RATE = 0.9
SQUARE_EPS = 1e-30
NORM_EPS = 1e-06
X = 4
MESH = pl.DeviceIdType.MESH
NT = (((1,), (1,)), ((), ()))
NN = (((1,), (0,)), ((), ()))


def kernel(
    S, Z, R, CA,
    x_hbm, cot_hbm, w_ref, gain_ref, row_ref, col_ref,
    out_hbm, step_ref, rown_ref, coln_ref, gg_ref,
    xs, gs, outs, wg, nt, lt, acc, gained, invs, gacc, wgf, rbuf, sbuf, tv, t1, t2,
    in_sem, lsem, out_sem, ag_s, ag_r, d_s, d_r, own_s, own_r, l_s, l_r,
    y_s, y_r, f_s, f_r, rs_s, rs_r, t_s, t_r,
):
    MICRO, TR, D = xs.shape
    SR = w_ref.shape[0]
    NC = Z * X
    H = TR // R
    U = MICRO * H
    NZP, NZM = Z // 2, Z // 2 - 1
    HB, HS = SR, SR // 2
    QW = min(256, D)
    NQ = D // QW
    s = lax.axis_index("section")
    dp = lax.axis_index("dp")
    z, x, c = dp // (2 * X), (dp // 2) % X, dp % 2

    def chip(dz, dx):
        return ((z + dz + Z) % Z) * X + (x + dx + X) % X

    def dev(dz, dx, flip=0):
        return (s, chip(dz, dx) * 2 + (c + flip) % 2)

    partner = dev(0, 0, 1)

    def remote(src, dst, ss, rs, device):
        return pltpu.make_async_remote_copy(
            src_ref=src, dst_ref=dst, send_sem=ss, recv_sem=rs, device_id=device, device_id_type=MESH
        )

    def load_x():
        return pltpu.make_async_copy(x_hbm, xs, in_sem.at[0])

    def load_cot():
        return pltpu.make_async_copy(cot_hbm, gs.at[:, pl.ds(0, TR)], in_sem.at[1])

    load_x().start()

    @pl.when(s == S - 1)
    def _():
        load_cot().start()

    own_row = pl.multiple_of(c * SR, SR)
    wg[chip(0, 0), pl.ds(own_row, SR), :] = w_ref[...]
    acc[...] = jnp.zeros_like(acc)
    gacc[...] = jnp.zeros_like(gacc)

    barrier = pltpu.get_barrier_semaphore()
    peers = [dev(0, k // 2, k % 2) for k in range(1, 2 * X)] + [dev(k, 0) for k in range(1, Z)]
    for p in peers:
        pl.semaphore_signal(barrier, inc=1, device_id=p, device_id_type=MESH)

    for ds in (1, S - 1):
        pl.semaphore_signal(barrier, inc=1, device_id=((s + ds) % S, dp), device_id_type=MESH)
    pl.semaphore_wait(barrier, len(peers) + 2)

    def nt_send(m):
        return remote(nt.at[m, :, 1 - c], lt.at[m, :, :, pl.ds(TR, TR)], l_s.at[m], l_r.at[m], partner)

    def nt_local(m):
        return pltpu.make_async_copy(nt.at[m, :, c], lt.at[m, :, :, pl.ds(0, TR)], lsem.at[m])

    def prepare(m):
        if m == 0:
            load_x().wait()
        total = jnp.zeros((TR, 1), jnp.float32)
        for q in range(NQ):
            part = xs[m, :, pl.ds(q * QW, QW)].astype(jnp.float32)
            total = total + jnp.sum(part * part, axis=-1, keepdims=True)
        inv = lax.rsqrt(total / D + NORM_EPS)
        invs[m] = jnp.broadcast_to(inv, invs.shape[1:])
        for q in range(NQ):
            cols = pl.ds(q * QW, QW)
            whitened = xs[m, :, cols].astype(jnp.float32) * inv
            normed = whitened * gain_ref[:, cols]
            n = QW // (2 * SR)
            nt[m, pl.ds(q * n, n)] = normed.T.astype(jnp.bfloat16).reshape(n, 2, SR, TR)
        nt_local(m).start()
        nt_send(m).start()

    def own_copy():
        rows = wg.at[chip(0, 0), pl.ds(own_row, SR)]
        return remote(rows, rows, own_s.at[0], own_r.at[0], partner)

    def gather(first, cols, other_cols, order):
        sent = []

        def blk(dz, dx, rows=pl.ds(0, 2 * SR)):
            return wg.at[chip(dz, dx), rows, cols]

        lo, hi = pl.ds(0, HB), pl.ds(HB, HB)

        def put(view, sem, device):
            copy = remote(view, view, ag_s.at[len(sent)], ag_r.at[sem], device)
            copy.start()
            sent.append(copy)

        dsent = []

        def across(view):
            copy = remote(view, view, d_s.at[len(dsent)], d_r.at[0], partner)
            copy.start()
            dsent.append(copy)

        def got(view, sem):
            remote(view, view, ag_s.at[0], ag_r.at[sem], partner).wait_recv()

        right, left, up, down = dev(0, 1), dev(0, -1), dev(1, 0), dev(-1, 0)
        fill = iter(range(MICRO))

        def filler():
            m = next(fill, None)
            if m is not None:
                prepare(m)

        if first == "z":
            zp = lambda k: k - 1
            zm = lambda k: NZP + k - 1
            base = Z - 1

            def x_out(i, rel):
                put(blk(rel, 0), base + 4 * i, right)
                put(blk(rel, 0), base + 4 * i + 1, left)
                if i:
                    across(blk(rel, 0))

            def x_mid(i, rel):
                got(blk(rel, -1), base + 4 * i)
                put(blk(rel, -1, lo), base + 4 * i + 2, right)
                across(blk(rel, -1))
                got(blk(rel, 1), base + 4 * i + 1)
                put(blk(rel, 1, hi), base + 4 * i + 3, left)
                across(blk(rel, 1))

            def x_end(i, rel):
                got(blk(rel, 2, lo), base + 4 * i + 2)
                got(blk(rel, 2, hi), base + 4 * i + 3)
                across(blk(rel, 2))

            put(blk(0, 0), zp(1), up)
            if NZM:
                put(blk(0, 0), zm(1), down)
            x_out(0, 0)
            filler()
            mids, ends, i = [(0, 0)], [], 0
            for k in range(1, NZP + 1):
                fresh = []
                got(blk(-k, 0), zp(k))
                if k < NZP:
                    put(blk(-k, 0), zp(k + 1), up)
                i += 1
                x_out(i, -k)
                fresh.append((i, -k))
                if k <= NZM:
                    got(blk(k, 0), zm(k))
                    if k < NZM:
                        put(blk(k, 0), zm(k + 1), down)
                    i += 1
                    x_out(i, k)
                    fresh.append((i, k))
                for pair in mids:
                    x_mid(*pair)
                for pair in ends:
                    x_end(*pair)
                mids, ends = fresh, mids
                filler()
            for pair in mids:
                x_mid(*pair)
            for pair in ends + mids:
                x_end(*pair)
        else:
            rels = [0, -1, 1, 2]
            hops = [(NZP, NZM), (NZM, NZP), (NZP, NZM), (NZM, NZP)]
            zp = lambda xi, k: 4 + xi * Z + k - 1
            zm = lambda xi, k: 4 + xi * Z + NZP + k - 1

            def z_out(xi):
                put(blk(0, rels[xi]), zp(xi, 1), up)
                put(blk(0, rels[xi]), zm(xi, 1), down)

            put(blk(0, 0), 0, right)
            put(blk(0, 0), 1, left)
            z_out(0)
            filler()
            got(blk(0, -1), 0)
            put(blk(0, -1, lo), 2, right)
            z_out(1)
            across(blk(0, -1))
            got(blk(0, 1), 1)
            put(blk(0, 1, hi), 3, left)
            z_out(2)
            across(blk(0, 1))
            filler()
            got(blk(0, 2, lo), 2)
            got(blk(0, 2, hi), 3)
            z_out(3)
            across(blk(0, 2))
            for k in range(1, NZP + 1):
                for xi in range(4):
                    most_p, most_m = hops[xi]
                    if k <= most_p:
                        got(blk(-k, rels[xi]), zp(xi, k))
                        if k < most_p:
                            put(blk(-k, rels[xi]), zp(xi, k + 1), up)
                        across(blk(-k, rels[xi]))
                    if k <= most_m:
                        got(blk(k, rels[xi]), zm(xi, k))
                        if k < most_m:
                            put(blk(k, rels[xi]), zm(xi, k + 1), down)
                        across(blk(k, rels[xi]))
                filler()
        while True:
            m = next(fill, None)
            if m is None:
                break
            prepare(m)
        whole = wg.at[pl.ds(0, NC - 1), :, other_cols]
        remote(whole, whole, d_s.at[0], d_r.at[0], partner).wait_recv()
        for copy in sent + dsent:
            copy.wait_send()

    own_copy().start()
    own_copy().wait_recv()
    cols_a, cols_b = pl.ds(0, CA), pl.ds(CA, D - CA)

    @pl.when(c == 0)
    def _():
        gather("z", cols_a, cols_b, None)

    @pl.when(c == 1)
    def _():
        gather("x", cols_b, cols_a, None)

    own_copy().wait_send()

    @pl.when(s == S - 1)
    def _():
        load_cot().wait()

    def hand_down(m, rows, u):
        return remote(outs.at[m, rows], gs.at[m, rows], y_s.at[u], y_r.at[u], (s - 1, dp))

    def share(m, h, u):
        rows = pl.ds(pl.multiple_of(h * R, R), R)
        there = pl.ds(pl.multiple_of(TR + h * R, R), R)
        return remote(gs.at[m, rows], gs.at[m, there], f_s.at[u], f_r.at[u], partner)

    def save(m):
        return pltpu.make_async_copy(outs.at[m], out_hbm.at[m], out_sem.at[m])

    def unit(m, h):
        u = m * H + h
        rows = pl.ds(h * R, R)

        @pl.when(s < S - 1)
        def _():
            hand_down(m, rows, u).wait_recv()

        share(m, h, u).start()
        g = gs[m, rows, :]
        inv = invs[m, rows, 0:1]
        dots = jnp.zeros((R, 1), jnp.float32)
        for q in range(NQ):
            cols = pl.ds(q * QW, QW)
            n = QW // (2 * SR)
            w = wg[pl.ds(q * n, n)].reshape(QW, D)
            branch = lax.dot_general(g, w, NT, preferred_element_type=jnp.float32)
            whitened = xs[m, rows, cols].astype(jnp.float32) * inv
            both = branch * whitened
            gacc[:, cols] += jnp.sum(both, axis=0, keepdims=True)
            dots = dots + jnp.sum(both * gain_ref[:, cols], axis=-1, keepdims=True)
            gained[:, cols] = branch * gain_ref[:, cols]
        mean = dots / D
        for q in range(NQ):
            cols = pl.ds(q * QW, QW)
            whitened = xs[m, rows, cols].astype(jnp.float32) * inv
            fresh = gs[m, rows, cols].astype(jnp.float32) + inv * (gained[:, cols] - whitened * mean)
            outs[m, rows, cols] = fresh.astype(jnp.bfloat16)

        @pl.when(s > 0)
        def _():
            hand_down(m, rows, u).start()

    def micro(m, carry):
        for h in range(H):
            unit(m, h)
        save(m).start()
        nt_local(m).wait()
        nt_send(m).wait_recv()
        for h in range(H):
            share(m, h, m * H + h).wait_recv()
        quarter = max(SR, NC * SR // 4)

        def part(r, carry):
            rows = pl.ds(pl.multiple_of(r * quarter, quarter), quarter)
            n = quarter // SR
            lhs = lt[m, pl.ds(r * n, n)].reshape(quarter, 2 * TR)
            acc[rows, :] += lax.dot_general(lhs, gs[m], NN, preferred_element_type=jnp.float32)
            return carry

        lax.fori_loop(0, NC * SR // quarter, part, 0)
        return carry

    lax.fori_loop(0, MICRO, micro, 0)

    def mine(dz, dx):
        return acc[pl.ds(pl.multiple_of(chip(dz, dx) * SR, SR), SR), :]

    def reduce(first):
        sent = []
        right, left, up, down = dev(0, 1), dev(0, -1), dev(1, 0), dev(-1, 0)
        lo, hi, full = pl.ds(0, HS), pl.ds(HS, HS), pl.ds(0, SR)

        def put(i, slot, sem, device, rows=full):
            copy = remote(sbuf.at[i, rows], rbuf.at[slot, rows], rs_s.at[len(sent)], rs_r.at[sem], device)
            copy.start()
            sent.append(copy)

        def got(slot, sem, rows=full):
            view = rbuf.at[slot, rows]
            remote(view, view, rs_s.at[0], rs_r.at[sem], partner).wait_recv()

        def taken(slot, rows=full):
            return rbuf[slot, rows, :].astype(jnp.float32)

        if first == "x":
            rels = []
            for k in range(NZP, 0, -1):
                rels.append(k)
                if k > 1:
                    rels.append(-(k - 1))
            rels.append(0)
            zslot, zsem = 3 * Z, 4 * Z

            def one(i):
                sbuf[3 * i] = mine(rels[i], 2).astype(jnp.bfloat16)
                put(3 * i, 3 * i, 4 * i, right, lo)
                put(3 * i, 3 * i, 4 * i + 1, left, hi)

            def two(i):
                got(3 * i, 4 * i, lo)
                value = mine(rels[i], 1)
                sbuf[3 * i + 1, lo, :] = (value[:HS] + taken(3 * i, lo)).astype(jnp.bfloat16)
                sbuf[3 * i + 1, hi, :] = value[HS:].astype(jnp.bfloat16)
                put(3 * i + 1, 3 * i + 1, 4 * i + 2, right)
                got(3 * i, 4 * i + 1, hi)
                value = mine(rels[i], -1)
                sbuf[3 * i + 2, lo, :] = value[:HS].astype(jnp.bfloat16)
                sbuf[3 * i + 2, hi, :] = (value[HS:] + taken(3 * i, hi)).astype(jnp.bfloat16)
                put(3 * i + 2, 3 * i + 2, 4 * i + 3, left)

            def three(i):
                rel = rels[i]
                got(3 * i + 1, 4 * i + 2)
                got(3 * i + 2, 4 * i + 3)
                value = mine(rel, 0) + taken(3 * i + 1) + taken(3 * i + 2)
                if rel > 0:
                    slot = zslot + rel - 1
                    if rel < NZP:
                        got(slot + 1, zsem + rel)
                        value = value + taken(slot + 1)
                    sbuf[slot] = value.astype(jnp.bfloat16)
                    put(slot, slot, zsem + rel - 1, up)
                elif rel < 0:
                    slot = zslot + NZP - rel - 1
                    if -rel < NZM:
                        got(slot + 1, zsem + NZP - rel)
                        value = value + taken(slot + 1)
                    sbuf[slot] = value.astype(jnp.bfloat16)
                    put(slot, slot, zsem + NZP - rel - 1, down)
                else:
                    got(zslot, zsem)
                    value = value + taken(zslot)
                    if NZM:
                        got(zslot + NZP, zsem + NZP)
                        value = value + taken(zslot + NZP)
                    wgf[...] = value

            for i in range(Z + 4):
                if i < Z:
                    one(i)
                if 0 <= i - 2 < Z:
                    two(i - 2)
                if 0 <= i - 4 < Z:
                    three(i - 4)
        else:
            rels = [2, 1, -1, 0]
            hops = [(NZP, NZM), (NZM, NZP), (NZP, NZM), (NZM, NZP)]
            zs = lambda xi, j: xi * (Z - 1) + j - 1
            xslot = 4 * (Z - 1)

            def link(xi, j, most, base, sign, device):
                value = mine(sign * j, rels[xi])
                slot = base + j - 1
                if j < most:
                    got(slot + 1, slot + 1)
                    value = value + taken(slot + 1)
                sbuf[slot] = value.astype(jnp.bfloat16)
                put(slot, slot, slot, device)

            def total(xi):
                most_p, most_m = hops[xi]
                base = xi * (Z - 1)
                value = mine(0, rels[xi])
                if most_p:
                    got(base, base)
                    value = value + taken(base)
                if most_m:
                    got(base + most_p, base + most_p)
                    value = value + taken(base + most_p)
                return value

            for t in range(NZP):
                for xi in range(4):
                    most_p, most_m = hops[xi]
                    base = xi * (Z - 1)
                    if most_p - t >= 1:
                        link(xi, most_p - t, most_p, base, 1, up)
                    if most_m - t >= 1:
                        link(xi, most_m - t, most_m, base + most_p, -1, down)
            sbuf[xslot] = total(0).astype(jnp.bfloat16)
            put(xslot, xslot, xslot, right, lo)
            put(xslot, xslot, xslot + 1, left, hi)
            ahead, behind = total(1), total(2)
            sbuf[xslot + 1, hi, :] = ahead[HS:].astype(jnp.bfloat16)
            sbuf[xslot + 2, lo, :] = behind[:HS].astype(jnp.bfloat16)
            got(xslot, xslot, lo)
            sbuf[xslot + 1, lo, :] = (ahead[:HS] + taken(xslot, lo)).astype(jnp.bfloat16)
            put(xslot + 1, xslot + 1, xslot + 2, right)
            got(xslot, xslot + 1, hi)
            sbuf[xslot + 2, hi, :] = (behind[HS:] + taken(xslot, hi)).astype(jnp.bfloat16)
            put(xslot + 2, xslot + 2, xslot + 3, left)
            value = total(3)
            got(xslot + 1, xslot + 2)
            got(xslot + 2, xslot + 3)
            wgf[...] = value + taken(xslot + 1) + taken(xslot + 2)
        for copy in sent:
            copy.wait_send()

    @pl.when(c == 0)
    def _():
        reduce("x")

    @pl.when(c == 1)
    def _():
        reduce("z")

    grad = wgf[...]
    row_sum = jnp.sum(grad * grad + SQUARE_EPS, axis=-1, keepdims=True)
    eye = lax.broadcasted_iota(jnp.int32, (SR, SR), 0) == lax.broadcasted_iota(jnp.int32, (SR, SR), 1)
    row_old = jnp.sum(jnp.where(eye, jnp.broadcast_to(row_ref[...], (SR, SR)), 0.0), axis=-1, keepdims=True)
    row_new = DECAY_RATE * row_old + (1.0 - DECAY_RATE) * (row_sum / D)
    rown_ref[...] = jnp.sum(jnp.where(eye, jnp.broadcast_to(row_new, (SR, SR)), 0.0), axis=0, keepdims=True)
    per_row = 1.0 / row_new
    tv[:, pl.ds(0, D)] = jnp.sum(grad * grad + SQUARE_EPS, axis=0, keepdims=True)
    tv[:, pl.ds(D, D)] = jnp.sum(grad * grad * per_row, axis=0, keepdims=True)
    tv[:, pl.ds(2 * D, D)] = gacc[...]
    tv[:, pl.ds(3 * D, 128)] = jnp.broadcast_to(jnp.sum(row_new, axis=0, keepdims=True), (1, 128))

    def spread(src, dst, place, targets, sem0):
        copies = [remote(src, dst.at[place], t_s.at[sem0 + k], t_r.at[sem0 + k], t) for k, t in enumerate(targets)]
        for copy in copies:
            copy.start()
        dst[place] = src[...]
        for copy in copies:
            copy.wait()
        total = dst[0]
        for k in range(1, dst.shape[0]):
            total = total + dst[k]
        return total

    tv[...] = spread(tv, t1, x * 2 + c, peers[: 2 * X - 1], 0)
    t2_src = tv
    sums = spread(t2_src, t2, z, peers[2 * X - 1 :], 2 * X - 1)
    col_new = DECAY_RATE * col_ref[...] + (1.0 - DECAY_RATE) * sums[:, 0:D] / D
    coln_ref[...] = col_new
    gg_ref[...] = sums[:, 2 * D : 3 * D]
    row_mean = sums[:, 3 * D : 3 * D + 1] / D
    total_square = row_mean * jnp.sum(sums[:, D : 2 * D] / col_new, axis=-1, keepdims=True)
    clip = jnp.maximum(1.0, jnp.sqrt(total_square / (D * D)))
    step_ref[...] = grad / jnp.sqrt(row_new * col_new / row_mean) / clip

    for m in range(MICRO):
        save(m).wait()
        nt_send(m).wait_send()

    def settle(u, carry):
        m, h = u // H, u % H
        share(m, h, u).wait_send()

        @pl.when(s > 0)
        def _():
            hand_down(m, pl.ds(pl.multiple_of(h * R, R), R), u).wait_send()

        return carry

    lax.fori_loop(0, U, settle, 0)


def body(saved_inputs, out_cotangent, weights, gains, row_state, col_state):
    S, DP = lax.axis_size("section"), lax.axis_size("dp")
    Z = DP // (2 * X)
    _, MICRO, TR, D = saved_inputs.shape
    SR = weights.shape[1]
    NC = DP // 2
    R = TR // 2
    CA = D // 2
    U = MICRO * (TR // R)
    bf, f32 = jnp.bfloat16, jnp.float32
    dma = pltpu.SemaphoreType.DMA
    vmem = pl.BlockSpec(memory_space=pltpu.VMEM)
    hbm = pl.BlockSpec(memory_space=pl.ANY)
    V = pltpu.VMEM
    scratch = [
        V((MICRO, TR, D), bf),
        V((MICRO, 2 * TR, D), bf),
        V((MICRO, TR, D), bf),
        V((NC, 2 * SR, D), bf),
        V((MICRO, NC, 2, SR, TR), bf),
        V((MICRO, NC, SR, 2 * TR), bf),
        V((NC * SR, D), f32),
        V((R, D), f32),
        V((MICRO, TR, 128), f32),
        V((1, D), f32),
        V((SR, D), f32),
        V((NC - 1, SR, D), bf),
        V((NC - 1, SR, D), bf),
        V((1, 3 * D + 128), f32),
        V((2 * X, 1, 3 * D + 128), f32),
        V((Z, 1, 3 * D + 128), f32),
        dma((2,)),
        dma((MICRO,)),
        dma((MICRO,)),
        dma((5 * Z,)),
        dma((5 * Z,)),
        dma((NC,)),
        dma((1,)),
        dma((1,)),
        dma((1,)),
        dma((MICRO,)),
        dma((MICRO,)),
        dma((U,)),
        dma((U,)),
        dma((U,)),
        dma((U,)),
        dma((5 * Z,)),
        dma((5 * Z,)),
        dma((2 * X + Z,)),
        dma((2 * X + Z,)),
    ]
    outs = pl.pallas_call(
        functools.partial(kernel, S, Z, R, CA),
        out_shape=(
            jax.ShapeDtypeStruct((MICRO, TR, D), bf),
            jax.ShapeDtypeStruct((SR, D), f32),
            jax.ShapeDtypeStruct((1, SR), f32),
            jax.ShapeDtypeStruct((1, D), f32),
            jax.ShapeDtypeStruct((1, D), f32),
        ),
        in_specs=[hbm, hbm, vmem, vmem, vmem, vmem],
        out_specs=(hbm, vmem, vmem, vmem, vmem),
        scratch_shapes=scratch,
        compiler_params=pltpu.CompilerParams(
            collective_id=0, has_side_effects=True, vmem_limit_bytes=60 * 2**20
        ),
        name="relay_back",
    )(saved_inputs[0], out_cotangent, weights[0], gains, row_state, col_state)
    return (outs[0][None], outs[1][None], outs[2], outs[3], outs[4])


def solution(mesh):
    placed = (
        P("section", None, "dp", None),
        P(None, "dp", None),
        P("section", "dp", None),
        P("section", None),
        P("section", "dp"),
        P("section", None),
    )
    return jax.shard_map(
        body,
        mesh=mesh,
        in_specs=placed,
        out_specs=(
            P("section", None, "dp", None),
            P("section", "dp", None),
            P("section", "dp"),
            P("section", None),
            P("section", None),
        ),
        check_vma=False,
    )
```

time: 758 us -> 170 us (0.22)
  waiting for transfers between devices: 377 us -> 0 us
  blocking collectives: 261 us -> 0 us
  Pallas kernels: 0 us -> 163 us
  other arithmetic: 46.7 us -> 0 us
  matrix products: 38.2 us -> 0 us
  between operations: 15.4 us -> 0.68 us
  starting transfers between devices: 9.04 us -> 0 us
    psum x2 -> x0, blocking collectives: 261 us -> none  [the longest x1 133 us: body(): lax.psum((jnp.sum(squares, axis=0), gain_sum, jnp.sum(row_fresh)), 'dp')]
    reduce_scatter x1 -> x0, waiting for transfers between devices: 185 us -> none  [body(): lax.psum_scatter(whole_term, 'dp', scatter_dimension=0, tiled=True)]
    pallas_call x0 -> x1, Pallas kernels: none -> 163 us  [body(): pl.pallas_call(functools.partial(kernel, S, Z, R, CA), out_shape=(jax.Sha...]
    ppermute x7 -> x0, waiting for transfers between devices: 102 us -> none  [from_behind(): return lax.ppermute(block, axis, route)]
    all_gather x1 -> x0, waiting for transfers between devices: 90 us -> none  [body(): full_weight = lax.all_gather(weights, 'dp', axis=1, tiled=True)[0]]
    dot_general x5 -> x0, matrix products: 38.2 us -> none  [the longest x4 25.7 us: section_back(): lax.dot_general(grad_out, full_weight, (((1,), (1,)), ((), ())), preferre...]
    dynamic_update_slice x14 -> x0, other arithmetic: 34.4 us -> none  [store_rows(): lax.dynamic_update_slice_in_dim(stored_rows, jnp.where(is_valid, fresh_ro...]
    ppermute x7 -> x0, starting transfers between devices: 8.96 us -> none  [from_behind(): return lax.ppermute(block, axis, route)]
  transfers between devices with their start and end apart: 9 -> 0, of which waited for: 9 -> 0; matrix products, arithmetic and copies ran while one was open for 0% -> 0% of each run, Pallas kernels for 0% -> 0%
where the time goes in v1:
time: 170 us
  Pallas kernels  163 us (96%)
  local copies, waits for them, and re-layouts  5.62 us (3%)
    pallas_call x1, Pallas kernels, body(): pl.pallas_call(functools.partial(kernel, S, Z, R, CA), out_shape=(jax.Sha...  163 us
    unnamed x13, local copies, waits for them, and re-layouts  5.62 us

profile of v1, /device:TPU:1, one launch (start us, length us, event | category | flops | bytes accessed | tf_op | source)
XLA Modules:
  0.0 169.6 jit_solution(1944157700628378923)
XLA Ops:
  0.6 163.3 %relay_back.1 = (bf16[4,128,2048]{2,1,0:T(8,128)(2,1)}, f32[32,2048]{1,0:T(8,128)}, f32[1,32]{1,0:T(1,128)}, f32[1,2048]{1,0:T(1,128)}, f32[1,2048]{1,0:T(1,128)}) custom-call(bf16[4,128,2048]{2,1,0:T(8,128)(2,1)} %bitcast.4, bf16[4,128,2048]{2,1,0:T(8,128)(2,1)} %cot_hbm.1, bf16[32,2048]{1,0:T(8,128)(2,1)} %bitcast.7, f32[1,2048]{1,0:T(1,128)} %gain_ref.1, ...), custom_call_target="tpu_custom_call" | custom-call | tf_op jit(solution)/shard_map/relay_back/pallas_call | solution.py:573
  163.9 0.0 copy-start
  163.9 0.0 copy-start.3
  163.9 0.0 copy-start.2
  164.0 0.0 copy-start.1
  164.0 3.2 %copy.16 = bf16[1,4,128,2048]{3,2,1,0:T(8,128)(2,1)} copy(bf16[1,4,128,2048]{3,2,1,0:T(8,128)(2,1)} %bitcast.5) | data formatting | bytes 4194304
  167.2 0.0 copy-done
  167.2 0.7 copy.17
  167.9 0.0 copy-done.3
  167.9 0.5 copy.18
  168.4 0.0 copy-done.2
  168.4 0.6 copy.19
  169.0 0.0 copy-done.1
  169.0 0.6 copy.20
Async XLA Ops:
  163.9 3.2 %copy-start = (f32[32,2048]{1,0:T(8,128)S(1)}, f32[32,2048]{1,0:T(8,128)}, u32[]{:S(2)}) copy-start(f32[32,2048]{1,0:T(8,128)} %get-tuple-element.11) | copy-start | bytes 786436
  163.9 3.9 %copy-start.3 = (f32[1,32]{1,0:T(1,128)S(1)}, f32[1,32]{1,0:T(1,128)}, u32[]{:S(2)}) copy-start(f32[1,32]{1,0:T(1,128)} %get-tuple-element.22) | copy-start | bytes 388
  163.9 4.4 %copy-start.2 = (f32[1,2048]{1,0:T(1,128)S(1)}, f32[1,2048]{1,0:T(1,128)}, u32[]{:S(2)}) copy-start(f32[1,2048]{1,0:T(1,128)} %get-tuple-element.23) | copy-start | bytes 24580
  164.0 5.0 %copy-start.1 = (f32[1,2048]{1,0:T(1,128)S(1)}, f32[1,2048]{1,0:T(1,128)}, u32[]{:S(2)}) copy-start(f32[1,2048]{1,0:T(1,128)} %get-tuple-element.24) | copy-start | bytes 24580

commit v2 on v1

--- a/solution.py
+++ b/solution.py
@@ -20,9 +20,9 @@
     S, Z, R, CA,
     x_hbm, cot_hbm, w_ref, gain_ref, row_ref, col_ref,
     out_hbm, step_ref, rown_ref, coln_ref, gg_ref,
-    xs, gs, outs, wg, nt, lt, acc, gained, invs, gacc, wgf, rbuf, sbuf, tv, t1, t2,
+    xs, gs, outs, wg, wt, nt, lt, acc, gained, invs, gacc, wgf, rbuf, sbuf, tv, t1, t2, gv, g1, g2,
     in_sem, lsem, out_sem, ag_s, ag_r, d_s, d_r, own_s, own_r, l_s, l_r,
-    y_s, y_r, f_s, f_r, rs_s, rs_r, t_s, t_r,
+    y_s, y_r, f_s, f_r, rs_s, rs_r, t_s, t_r, g_s, g_r,
 ):
     MICRO, TR, D = xs.shape
     SR = w_ref.shape[0]
@@ -64,8 +64,6 @@
 
     own_row = pl.multiple_of(c * SR, SR)
     wg[chip(0, 0), pl.ds(own_row, SR), :] = w_ref[...]
-    acc[...] = jnp.zeros_like(acc)
-    gacc[...] = jnp.zeros_like(gacc)
 
     barrier = pltpu.get_barrier_semaphore()
     peers = [dev(0, k // 2, k % 2) for k in range(1, 2 * X)] + [dev(k, 0) for k in range(1, Z)]
@@ -105,24 +103,31 @@
         return remote(rows, rows, own_s.at[0], own_r.at[0], partner)
 
     def gather(first, cols, other_cols, order):
-        sent = []
-
         def blk(dz, dx, rows=pl.ds(0, 2 * SR)):
             return wg.at[chip(dz, dx), rows, cols]
 
         lo, hi = pl.ds(0, HB), pl.ds(HB, HB)
 
         def put(view, sem, device):
-            copy = remote(view, view, ag_s.at[len(sent)], ag_r.at[sem], device)
-            copy.start()
-            sent.append(copy)
-
-        dsent = []
-
-        def across(view):
-            copy = remote(view, view, d_s.at[len(dsent)], d_r.at[0], partner)
-            copy.start()
-            dsent.append(copy)
+            remote(view, view, ag_s.at[0], ag_r.at[sem], device).start()
+
+        def across(view, i):
+            remote(view, view, d_s.at[0], d_r.at[i], partner).start()
+
+        def group(i):
+            return 0 if i == 0 else (-(i + 1) // 2 if i % 2 else i // 2)
+
+        def flip(i, part):
+            first_chip = ((z + group(i) + Z) % Z) * X
+            block = wg[pl.ds(first_chip, X), :, part].reshape(X * 2 * SR, part.size)
+            width = X * 2 * SR
+            wt[part, pl.ds(pl.multiple_of(first_chip * 2 * SR, width), width)] = block.T
+
+        def flip_other(i):
+            n = X if i else X - 1
+            whole = wg.at[pl.ds(0, n), :, other_cols]
+            remote(whole, whole, d_s.at[0], d_r.at[i], partner).wait_recv()
+            flip(i, other_cols)
 
         def got(view, sem):
             remote(view, view, ag_s.at[0], ag_r.at[sem], partner).wait_recv()
@@ -134,6 +139,10 @@
             m = next(fill, None)
             if m is not None:
                 prepare(m)
+                rows = pl.ds(m * (NC * SR // MICRO), NC * SR // MICRO)
+                acc[rows, :] = jnp.zeros((NC * SR // MICRO, D), jnp.float32)
+            if m == 0:
+                gacc[...] = jnp.zeros_like(gacc)
 
         if first == "z":
             zp = lambda k: k - 1
@@ -144,20 +153,21 @@
                 put(blk(rel, 0), base + 4 * i, right)
                 put(blk(rel, 0), base + 4 * i + 1, left)
                 if i:
-                    across(blk(rel, 0))
+                    across(blk(rel, 0), i)
 
             def x_mid(i, rel):
                 got(blk(rel, -1), base + 4 * i)
                 put(blk(rel, -1, lo), base + 4 * i + 2, right)
-                across(blk(rel, -1))
+                across(blk(rel, -1), i)
                 got(blk(rel, 1), base + 4 * i + 1)
                 put(blk(rel, 1, hi), base + 4 * i + 3, left)
-                across(blk(rel, 1))
+                across(blk(rel, 1), i)
 
             def x_end(i, rel):
                 got(blk(rel, 2, lo), base + 4 * i + 2)
                 got(blk(rel, 2, hi), base + 4 * i + 3)
-                across(blk(rel, 2))
+                across(blk(rel, 2), i)
+                flip(i, cols)
 
             put(blk(0, 0), zp(1), up)
             if NZM:
@@ -188,8 +198,14 @@
                 filler()
             for pair in mids:
                 x_mid(*pair)
-            for pair in ends + mids:
+            for pair in ends:
                 x_end(*pair)
+            for i in range(Z - 3):
+                flip_other(i)
+            for pair in mids:
+                x_end(*pair)
+            for i in range(Z - 3, Z):
+                flip_other(i)
         else:
             rels = [0, -1, 1, 2]
             hops = [(NZP, NZM), (NZM, NZP), (NZP, NZM), (NZM, NZP)]
@@ -207,16 +223,18 @@
             got(blk(0, -1), 0)
             put(blk(0, -1, lo), 2, right)
             z_out(1)
-            across(blk(0, -1))
+            across(blk(0, -1), 0)
             got(blk(0, 1), 1)
             put(blk(0, 1, hi), 3, left)
             z_out(2)
-            across(blk(0, 1))
+            across(blk(0, 1), 0)
             filler()
             got(blk(0, 2, lo), 2)
             got(blk(0, 2, hi), 3)
             z_out(3)
-            across(blk(0, 2))
+            across(blk(0, 2), 0)
+            flip(0, cols)
+            flipped = 0
             for k in range(1, NZP + 1):
                 for xi in range(4):
                     most_p, most_m = hops[xi]
@@ -224,22 +242,27 @@
                         got(blk(-k, rels[xi]), zp(xi, k))
                         if k < most_p:
                             put(blk(-k, rels[xi]), zp(xi, k + 1), up)
-                        across(blk(-k, rels[xi]))
+                        across(blk(-k, rels[xi]), 2 * k - 1)
                     if k <= most_m:
                         got(blk(k, rels[xi]), zm(xi, k))
                         if k < most_m:
                             put(blk(k, rels[xi]), zm(xi, k + 1), down)
-                        across(blk(k, rels[xi]))
+                        across(blk(k, rels[xi]), 2 * k if k < NZP else 2 * k - 1)
+                flip(2 * k - 1, cols)
+                if k < NZP:
+                    flip(2 * k, cols)
+                if k > 2:
+                    flip_other(flipped)
+                    flip_other(flipped + 1)
+                    flipped += 2
                 filler()
-        while True:
-            m = next(fill, None)
-            if m is None:
-                break
-            prepare(m)
-        whole = wg.at[pl.ds(0, NC - 1), :, other_cols]
-        remote(whole, whole, d_s.at[0], d_r.at[0], partner).wait_recv()
-        for copy in sent + dsent:
-            copy.wait_send()
+            for i in range(flipped, Z):
+                flip_other(i)
+        for _ in range(MICRO):
+            filler()
+        everything = wg.at[pl.ds(0, NC - 1), :, cols]
+        remote(everything, everything, ag_s.at[0], ag_r.at[0], partner).wait_send()
+        remote(everything, everything, d_s.at[0], d_r.at[0], partner).wait_send()
 
     own_copy().start()
     own_copy().wait_recv()
@@ -260,36 +283,28 @@
         load_cot().wait()
 
     def hand_down(m, rows, u):
-        return remote(outs.at[m, rows], gs.at[m, rows], y_s.at[u], y_r.at[u], (s - 1, dp))
-
-    def share(m, h, u):
-        rows = pl.ds(pl.multiple_of(h * R, R), R)
-        there = pl.ds(pl.multiple_of(TR + h * R, R), R)
-        return remote(gs.at[m, rows], gs.at[m, there], f_s.at[u], f_r.at[u], partner)
-
-    def save(m):
-        return pltpu.make_async_copy(outs.at[m], out_hbm.at[m], out_sem.at[m])
-
-    def unit(m, h):
-        u = m * H + h
-        rows = pl.ds(h * R, R)
-
-        @pl.when(s < S - 1)
-        def _():
-            hand_down(m, rows, u).wait_recv()
-
-        share(m, h, u).start()
+        return remote(outs.at[m, rows], gs.at[m, rows], y_s.at[0], y_r.at[u], (s - 1, dp))
+
+    def share(m, rows, there):
+        return remote(gs.at[m, rows], gs.at[m, there], f_s.at[0], f_r.at[m], partner)
+
+    def save():
+        return pltpu.make_async_copy(outs, out_hbm, out_sem.at[0])
+
+    def place(u, base=0):
+        return u // H, pl.ds(pl.multiple_of(base + (u % H) * R, R), R)
+
+    def differentiate(u):
+        m, rows = place(u)
         g = gs[m, rows, :]
         inv = invs[m, rows, 0:1]
         dots = jnp.zeros((R, 1), jnp.float32)
         for q in range(NQ):
             cols = pl.ds(q * QW, QW)
-            n = QW // (2 * SR)
-            w = wg[pl.ds(q * n, n)].reshape(QW, D)
-            branch = lax.dot_general(g, w, NT, preferred_element_type=jnp.float32)
+            branch = lax.dot_general(g, wt[:, cols], NN, preferred_element_type=jnp.float32)
             whitened = xs[m, rows, cols].astype(jnp.float32) * inv
             both = branch * whitened
-            gacc[:, cols] += jnp.sum(both, axis=0, keepdims=True)
+            gacc[:, cols] += jnp.sum(both.reshape(R // 8, 8, QW), axis=0)
             dots = dots + jnp.sum(both * gain_ref[:, cols], axis=-1, keepdims=True)
             gained[:, cols] = branch * gain_ref[:, cols]
         mean = dots / D
@@ -299,44 +314,102 @@
             fresh = gs[m, rows, cols].astype(jnp.float32) + inv * (gained[:, cols] - whitened * mean)
             outs[m, rows, cols] = fresh.astype(jnp.bfloat16)
 
+    quarter = NC * SR // H
+
+    def weigh(m, r):
+        rows = pl.ds(pl.multiple_of(r * quarter, quarter), quarter)
+        n = quarter // SR
+        lhs = lt[m, pl.ds(r * n, n)].reshape(quarter, 2 * TR)
+        acc[rows, :] += lax.dot_general(lhs, gs[m], NN, preferred_element_type=jnp.float32)
+
+    def meet(m):
+        nt_local(m).wait()
+        nt_send(m).wait_recv()
+        share(m, pl.ds(0, TR), pl.ds(TR, TR)).wait_recv()
+
+    lag = jnp.where(s == 0, 1, 0)
+
+    def tick(u, carry):
+        m, rows = place(u)
+
+        @pl.when(s < S - 1)
+        def _():
+            hand_down(m, rows, u).wait_recv()
+
+        share(m, rows, place(u, TR)[1]).start()
+
+        @pl.when(u >= lag)
+        def _():
+            differentiate(u - lag)
+
         @pl.when(s > 0)
         def _():
             hand_down(m, rows, u).start()
 
-    def micro(m, carry):
-        for h in range(H):
-            unit(m, h)
-        save(m).start()
-        nt_local(m).wait()
-        nt_send(m).wait_recv()
-        for h in range(H):
-            share(m, h, m * H + h).wait_recv()
-        quarter = max(SR, NC * SR // 4)
-
-        def part(r, carry):
-            rows = pl.ds(pl.multiple_of(r * quarter, quarter), quarter)
-            n = quarter // SR
-            lhs = lt[m, pl.ds(r * n, n)].reshape(quarter, 2 * TR)
-            acc[rows, :] += lax.dot_general(lhs, gs[m], NN, preferred_element_type=jnp.float32)
-            return carry
-
-        lax.fori_loop(0, NC * SR // quarter, part, 0)
+        @pl.when(u >= H)
+        def _():
+            @pl.when(u % H == 0)
+            def _():
+                meet(m - 1)
+
+            weigh(m - 1, u % H)
+
         return carry
 
-    lax.fori_loop(0, MICRO, micro, 0)
+    lax.fori_loop(0, U, tick, 0)
+    meet(MICRO - 1)
+
+    def last(r, carry):
+        weigh(MICRO - 1, r)
+        return carry
+
+    lax.fori_loop(0, H, last, 0)
+
+    def spread(src, dst, place, targets, ss, rs, sem0):
+        return [remote(src, dst.at[place], ss.at[sem0 + k], rs.at[sem0 + k], t) for k, t in enumerate(targets)]
+
+    def added(dst):
+        total = dst[0]
+        for k in range(1, dst.shape[0]):
+            total = total + dst[k]
+        return total
+
+    near, far = peers[: 2 * X - 1], peers[2 * X - 1 :]
+
+    def gain_near():
+        return spread(gv.at[0], g1, x * 2 + c, near, g_s, g_r, 0)
+
+    def gain_far():
+        return spread(gv.at[1], g2, z, far, g_s, g_r, 2 * X - 1)
+
+    def hook_a():
+        @pl.when(s == 0)
+        def _():
+            differentiate(U - 1)
+
+        save().start()
+        gv[0] = jnp.sum(gacc[...], axis=0, keepdims=True)
+        for copy in gain_near():
+            copy.start()
+        g1[x * 2 + c] = gv[0]
+
+    def hook_b():
+        for copy in gain_near():
+            copy.wait_recv()
+        gv[1] = added(g1)
+        for copy in gain_far():
+            copy.start()
+        g2[z] = gv[1]
 
     def mine(dz, dx):
         return acc[pl.ds(pl.multiple_of(chip(dz, dx) * SR, SR), SR), :]
 
     def reduce(first):
-        sent = []
         right, left, up, down = dev(0, 1), dev(0, -1), dev(1, 0), dev(-1, 0)
         lo, hi, full = pl.ds(0, HS), pl.ds(HS, HS), pl.ds(0, SR)
 
         def put(i, slot, sem, device, rows=full):
-            copy = remote(sbuf.at[i, rows], rbuf.at[slot, rows], rs_s.at[len(sent)], rs_r.at[sem], device)
-            copy.start()
-            sent.append(copy)
+            remote(sbuf.at[i, rows], rbuf.at[slot, rows], rs_s.at[0], rs_r.at[sem], device).start()
 
         def got(slot, sem, rows=full):
             view = rbuf.at[slot, rows]
@@ -405,6 +478,10 @@
                     two(i - 2)
                 if 0 <= i - 4 < Z:
                     three(i - 4)
+                if i == 2:
+                    hook_a()
+                if i == Z:
+                    hook_b()
         else:
             rels = [2, 1, -1, 0]
             hops = [(NZP, NZM), (NZM, NZP), (NZP, NZM), (NZM, NZP)]
@@ -440,6 +517,10 @@
                         link(xi, most_p - t, most_p, base, 1, up)
                     if most_m - t >= 1:
                         link(xi, most_m - t, most_m, base + most_p, -1, down)
+                if t == 0:
+                    hook_a()
+                if t == NZP - 1:
+                    hook_b()
             sbuf[xslot] = total(0).astype(jnp.bfloat16)
             put(xslot, xslot, xslot, right, lo)
             put(xslot, xslot, xslot + 1, left, hi)
@@ -456,8 +537,7 @@
             got(xslot + 1, xslot + 2)
             got(xslot + 2, xslot + 3)
             wgf[...] = value + taken(xslot + 1) + taken(xslot + 2)
-        for copy in sent:
-            copy.wait_send()
+        remote(sbuf, rbuf, rs_s.at[0], rs_r.at[0], partner).wait_send()
 
     @pl.when(c == 0)
     def _():
@@ -474,49 +554,59 @@
     row_new = DECAY_RATE * row_old + (1.0 - DECAY_RATE) * (row_sum / D)
     rown_ref[...] = jnp.sum(jnp.where(eye, jnp.broadcast_to(row_new, (SR, SR)), 0.0), axis=0, keepdims=True)
     per_row = 1.0 / row_new
-    tv[:, pl.ds(0, D)] = jnp.sum(grad * grad + SQUARE_EPS, axis=0, keepdims=True)
-    tv[:, pl.ds(D, D)] = jnp.sum(grad * grad * per_row, axis=0, keepdims=True)
-    tv[:, pl.ds(2 * D, D)] = gacc[...]
-    tv[:, pl.ds(3 * D, 128)] = jnp.broadcast_to(jnp.sum(row_new, axis=0, keepdims=True), (1, 128))
-
-    def spread(src, dst, place, targets, sem0):
-        copies = [remote(src, dst.at[place], t_s.at[sem0 + k], t_r.at[sem0 + k], t) for k, t in enumerate(targets)]
+    tv[0, :, pl.ds(0, D)] = jnp.sum(grad * grad + SQUARE_EPS, axis=0, keepdims=True)
+    tv[0, :, pl.ds(D, D)] = jnp.sum(grad * grad * per_row, axis=0, keepdims=True)
+    tv[0, :, pl.ds(2 * D, 128)] = jnp.broadcast_to(jnp.sum(row_new, axis=0, keepdims=True), (1, 128))
+
+    def exchange(copies, dst, place, value):
         for copy in copies:
             copy.start()
-        dst[place] = src[...]
+        dst[place] = value
         for copy in copies:
-            copy.wait()
-        total = dst[0]
-        for k in range(1, dst.shape[0]):
-            total = total + dst[k]
-        return total
-
-    tv[...] = spread(tv, t1, x * 2 + c, peers[: 2 * X - 1], 0)
-    t2_src = tv
-    sums = spread(t2_src, t2, z, peers[2 * X - 1 :], 2 * X - 1)
+            copy.wait_recv()
+        return added(dst)
+
+    near_copies = spread(tv.at[0], t1, x * 2 + c, near, t_s, t_r, 0)
+    far_copies = spread(tv.at[1], t2, z, far, t_s, t_r, 2 * X - 1)
+    tv[1] = exchange(near_copies, t1, x * 2 + c, tv[0])
+    sums = exchange(far_copies, t2, z, tv[1])
     col_new = DECAY_RATE * col_ref[...] + (1.0 - DECAY_RATE) * sums[:, 0:D] / D
     coln_ref[...] = col_new
-    gg_ref[...] = sums[:, 2 * D : 3 * D]
-    row_mean = sums[:, 3 * D : 3 * D + 1] / D
+    row_mean = sums[:, 2 * D : 2 * D + 1] / D
     total_square = row_mean * jnp.sum(sums[:, D : 2 * D] / col_new, axis=-1, keepdims=True)
     clip = jnp.maximum(1.0, jnp.sqrt(total_square / (D * D)))
     step_ref[...] = grad / jnp.sqrt(row_new * col_new / row_mean) / clip
-
+    for copy in gain_far():
+        copy.wait_recv()
+    gg_ref[...] = added(g2)
+
+    for copy in near_copies + far_copies + gain_near() + gain_far():
+        copy.wait_send()
+    save().wait()
     for m in range(MICRO):
-        save(m).wait()
         nt_send(m).wait_send()
-
-    def settle(u, carry):
-        m, h = u // H, u % H
-        share(m, h, u).wait_send()
-
-        @pl.when(s > 0)
-        def _():
-            hand_down(m, pl.ds(pl.multiple_of(h * R, R), R), u).wait_send()
-
-        return carry
-
-    lax.fori_loop(0, U, settle, 0)
+    shared = gs.at[:, pl.ds(0, TR)]
+    remote(shared, shared, f_s.at[0], f_r.at[0], partner).wait_send()
+
+    @pl.when(s > 0)
+    def _():
+        remote(outs, outs, y_s.at[0], y_r.at[0], partner).wait_send()
+
+
+def deliver(*refs):
+    n = len(refs) // 2
+    sems = refs[-1]
+    sources, results = refs[:n], refs[n : 2 * n]
+    copies = []
+    for src, dst in zip(sources, results):
+        pieces = src.shape[0] if len(src.shape) == 3 else 1
+        for k in range(pieces):
+            a, b = (src.at[k], dst.at[k]) if pieces > 1 else (src, dst)
+            copies.append(pltpu.make_async_copy(a, b, sems.at[len(copies)]))
+    for copy in copies:
+        copy.start()
+    for copy in copies:
+        copy.wait()
 
 
 def body(saved_inputs, out_cotangent, weights, gains, row_state, col_state):
@@ -525,8 +615,8 @@
     _, MICRO, TR, D = saved_inputs.shape
     SR = weights.shape[1]
     NC = DP // 2
-    R = TR // 2
-    CA = D // 2
+    R = TR // 4
+    CA = D * 9 // 16
     U = MICRO * (TR // R)
     bf, f32 = jnp.bfloat16, jnp.float32
     dma = pltpu.SemaphoreType.DMA
@@ -538,35 +628,41 @@
         V((MICRO, 2 * TR, D), bf),
         V((MICRO, TR, D), bf),
         V((NC, 2 * SR, D), bf),
+        V((D, D), bf),
         V((MICRO, NC, 2, SR, TR), bf),
         V((MICRO, NC, SR, 2 * TR), bf),
         V((NC * SR, D), f32),
         V((R, D), f32),
         V((MICRO, TR, 128), f32),
-        V((1, D), f32),
+        V((8, D), f32),
         V((SR, D), f32),
         V((NC - 1, SR, D), bf),
         V((NC - 1, SR, D), bf),
-        V((1, 3 * D + 128), f32),
-        V((2 * X, 1, 3 * D + 128), f32),
-        V((Z, 1, 3 * D + 128), f32),
+        V((2, 1, 2 * D + 128), f32),
+        V((2 * X, 1, 2 * D + 128), f32),
+        V((Z, 1, 2 * D + 128), f32),
+        V((2, 1, D), f32),
+        V((2 * X, 1, D), f32),
+        V((Z, 1, D), f32),
         dma((2,)),
         dma((MICRO,)),
-        dma((MICRO,)),
+        dma((1,)),
+        dma((1,)),
         dma((5 * Z,)),
-        dma((5 * Z,)),
-        dma((NC,)),
         dma((1,)),
+        dma((Z,)),
         dma((1,)),
         dma((1,)),
         dma((MICRO,)),
         dma((MICRO,)),
+        dma((1,)),
         dma((U,)),
-        dma((U,)),
-        dma((U,)),
-        dma((U,)),
+        dma((1,)),
+        dma((MICRO,)),
+        dma((1,)),
         dma((5 * Z,)),
-        dma((5 * Z,)),
+        dma((2 * X + Z,)),
+        dma((2 * X + Z,)),
         dma((2 * X + Z,)),
         dma((2 * X + Z,)),
     ]
@@ -587,6 +683,14 @@
         ),
         name="relay_back",
     )(saved_inputs[0], out_cotangent, weights[0], gains, row_state, col_state)
+    outs = pl.pallas_call(
+        deliver,
+        out_shape=tuple(jax.ShapeDtypeStruct(o.shape, o.dtype) for o in outs),
+        in_specs=[hbm] * 5,
+        out_specs=(hbm,) * 5,
+        scratch_shapes=[dma((MICRO + 4,))],
+        name="deliver",
+    )(*outs)
     return (outs[0][None], outs[1][None], outs[2], outs[3], outs[4])
 
 

time: 170 us -> 226 us (1.33)
  Pallas kernels: 163 us -> 225 us
  local copies, waits for them, and re-layouts: 5.62 us -> 0 us
    pallas_call x0 -> x1, Pallas kernels: none -> 73.2 us  [body(): pl.pallas_call(deliver, out_shape=tuple((jax.ShapeDtypeStruct(o.shape, o....]
    pallas_call x1, Pallas kernels: 163 us -> 152 us  [body(): pl.pallas_call(functools.partial(kernel, S, Z, R, CA), out_shape=(jax.Sha...]
    unnamed x13 -> x0, local copies, waits for them, and re-layouts: 5.62 us -> none
where the time goes in v2:
time: 226 us
  Pallas kernels  225 us (100%)
    pallas_call x1, Pallas kernels, body(): pl.pallas_call(functools.partial(kernel, S, Z, R, CA), out_shape=(jax.Sha...  152 us
    pallas_call x1, Pallas kernels, body(): pl.pallas_call(deliver, out_shape=tuple((jax.ShapeDtypeStruct(o.shape, o....  73.2 us

profile of v2, /device:TPU:1, one launch (start us, length us, event | category | flops | bytes accessed | tf_op | source)
XLA Modules:
  0.0 226.3 jit_solution(8537438447468295552)
XLA Ops:
  0.6 152.3 %relay_back.1 = (bf16[4,128,2048]{2,1,0:T(8,128)(2,1)}, f32[32,2048]{1,0:T(8,128)}, f32[1,32]{1,0:T(1,128)}, f32[1,2048]{1,0:T(1,128)}, f32[1,2048]{1,0:T(1,128)}) custom-call(bf16[4,128,2048]{2,1,0:T(8,128)(2,1)} %bitcast.4, bf16[4,128,2048]{2,1,0:T(8,128)(2,1)} %cot_hbm.1, bf16[32,2048]{1,0:T(8,128)(2,1)} %bitcast.5, f32[1,2048]{1,0:T(1,128)} %gain_ref.1, ...), custom_call_target="tpu_custom_call" | custom-call | tf_op jit(solution)/shard_map/relay_back/pallas_call | solution.py:669
  152.9 73.2 %deliver.1 = (bf16[4,128,2048]{2,1,0:T(8,128)(2,1)}, f32[32,2048]{1,0:T(8,128)}, f32[1,32]{1,0:T(1,128)}, f32[1,2048]{1,0:T(1,128)}, f32[1,2048]{1,0:T(1,128)}) custom-call(bf16[4,128,2048]{2,1,0:T(8,128)(2,1)} %get-tuple-element.15.refs_0_, f32[32,2048]{1,0:T(8,128)} %get-tuple-element.16.refs_1_, f32[1,32]{1,0:T(1,128)} %get-tuple-element.17.refs_2_, ...), custom_call_target="tpu_custom_call" | custom-call | tf_op jit(solution)/shard_map/deliver/pallas_call | solution.py:686

commit v3 on v2

--- a/solution.py
+++ b/solution.py
@@ -594,19 +594,27 @@
 
 
 def deliver(*refs):
-    n = len(refs) // 2
-    sems = refs[-1]
-    sources, results = refs[:n], refs[n : 2 * n]
-    copies = []
-    for src, dst in zip(sources, results):
+    n = 5
+    sources, results, held, sems = refs[:n], refs[n : 2 * n], refs[2 * n : 3 * n], refs[-1]
+    ways = []
+    for src, mid, dst in zip(sources, held, results):
         pieces = src.shape[0] if len(src.shape) == 3 else 1
         for k in range(pieces):
-            a, b = (src.at[k], dst.at[k]) if pieces > 1 else (src, dst)
-            copies.append(pltpu.make_async_copy(a, b, sems.at[len(copies)]))
-    for copy in copies:
-        copy.start()
-    for copy in copies:
-        copy.wait()
+            a, m, b = (src.at[k], mid.at[k], dst.at[k]) if pieces > 1 else (src, mid, dst)
+            i = len(ways)
+            ways.append(
+                (
+                    pltpu.make_async_copy(a, m, sems.at[0, i]),
+                    pltpu.make_async_copy(m, b, sems.at[1, i]),
+                )
+            )
+    for into, _ in ways:
+        into.start()
+    for into, out in ways:
+        into.wait()
+        out.start()
+    for _, out in ways:
+        out.wait()
 
 
 def body(saved_inputs, out_cotangent, weights, gains, row_state, col_state):
@@ -688,7 +696,7 @@
         out_shape=tuple(jax.ShapeDtypeStruct(o.shape, o.dtype) for o in outs),
         in_specs=[hbm] * 5,
         out_specs=(hbm,) * 5,
-        scratch_shapes=[dma((MICRO + 4,))],
+        scratch_shapes=[V(o.shape, o.dtype) for o in outs] + [dma((2, MICRO + 4))],
         name="deliver",
     )(*outs)
     return (outs[0][None], outs[1][None], outs[2], outs[3], outs[4])

time: 226 us -> 156 us (0.69)
  Pallas kernels: 225 us -> 155 us
    pallas_call x1, Pallas kernels: 73.2 us -> 2.58 us  [body(): pl.pallas_call(deliver, out_shape=tuple((jax.ShapeDtypeStruct(o.shape, o....]
where the time goes in v3:
time: 156 us
  Pallas kernels  155 us (99%)
    pallas_call x1, Pallas kernels, body(): pl.pallas_call(functools.partial(kernel, S, Z, R, CA), out_shape=(jax.Sha...  152 us

profile of v3, /device:TPU:1, one launch (start us, length us, event | category | flops | bytes accessed | tf_op | source)
XLA Modules:
  0.0 155.7 jit_solution(16565388306116357027)
XLA Ops:
  0.6 152.3 %relay_back.1 = (bf16[4,128,2048]{2,1,0:T(8,128)(2,1)}, f32[32,2048]{1,0:T(8,128)}, f32[1,32]{1,0:T(1,128)}, f32[1,2048]{1,0:T(1,128)}, f32[1,2048]{1,0:T(1,128)}) custom-call(bf16[4,128,2048]{2,1,0:T(8,128)(2,1)} %bitcast.4, bf16[4,128,2048]{2,1,0:T(8,128)(2,1)} %cot_hbm.1, bf16[32,2048]{1,0:T(8,128)(2,1)} %bitcast.5, f32[1,2048]{1,0:T(1,128)} %gain_ref.1, ...), custom_call_target="tpu_custom_call" | custom-call | tf_op jit(solution)/shard_map/relay_back/pallas_call | solution.py:677
  152.9 2.6 %deliver.1 = (bf16[4,128,2048]{2,1,0:T(8,128)(2,1)}, f32[32,2048]{1,0:T(8,128)}, f32[1,32]{1,0:T(1,128)}, f32[1,2048]{1,0:T(1,128)}, f32[1,2048]{1,0:T(1,128)}) custom-call(bf16[4,128,2048]{2,1,0:T(8,128)(2,1)} %get-tuple-element.15.refs_0_, f32[32,2048]{1,0:T(8,128)} %get-tuple-element.16.refs_1_, f32[1,32]{1,0:T(1,128)} %get-tuple-element.17.refs_2_, ...), custom_call_target="tpu_custom_call" | custom-call | tf_op jit(solution)/shard_map/deliver/pallas_call | solution.py:694

commit v4 on v3

--- a/solution.py
+++ b/solution.py
@@ -20,7 +20,7 @@
     S, Z, R, CA,
     x_hbm, cot_hbm, w_ref, gain_ref, row_ref, col_ref,
     out_hbm, step_ref, rown_ref, coln_ref, gg_ref,
-    xs, gs, outs, wg, wt, nt, lt, acc, gained, invs, gacc, wgf, rbuf, sbuf, tv, t1, t2, gv, g1, g2,
+    xs, gs, outs, wg, wt, nt, lt, acc, gained, invs, gacc, wgf, rbuf, sbuf, tv, t1, tu, t2, tw, t3, gv, g1, g2,
     in_sem, lsem, out_sem, ag_s, ag_r, d_s, d_r, own_s, own_r, l_s, l_r,
     y_s, y_r, f_s, f_r, rs_s, rs_r, t_s, t_r, g_s, g_r,
 ):
@@ -63,6 +63,7 @@
         load_cot().start()
 
     own_row = pl.multiple_of(c * SR, SR)
+    other_row = pl.multiple_of((1 - c) * SR, SR)
     wg[chip(0, 0), pl.ds(own_row, SR), :] = w_ref[...]
 
     barrier = pltpu.get_barrier_semaphore()
@@ -114,6 +115,10 @@
         def across(view, i):
             remote(view, view, d_s.at[0], d_r.at[i], partner).start()
 
+        def put_own(base_rows, places):
+            for sem, device in places:
+                put(blk(0, 0, pl.ds(base_rows, SR)), sem, device)
+
         def group(i):
             return 0 if i == 0 else (-(i + 1) // 2 if i % 2 else i // 2)
 
@@ -152,8 +157,7 @@
             def x_out(i, rel):
                 put(blk(rel, 0), base + 4 * i, right)
                 put(blk(rel, 0), base + 4 * i + 1, left)
-                if i:
-                    across(blk(rel, 0), i)
+                across(blk(rel, 0), i)
 
             def x_mid(i, rel):
                 got(blk(rel, -1), base + 4 * i)
@@ -169,10 +173,12 @@
                 across(blk(rel, 2), i)
                 flip(i, cols)
 
-            put(blk(0, 0), zp(1), up)
+            places = [(zp(1), up), (base, right), (base + 1, left)]
             if NZM:
-                put(blk(0, 0), zm(1), down)
-            x_out(0, 0)
+                places.insert(1, (zm(1), down))
+            put_own(own_row, places)
+            own_copy().wait_recv()
+            put_own(other_row, places)
             filler()
             mids, ends, i = [(0, 0)], [], 0
             for k in range(1, NZP + 1):
@@ -216,9 +222,10 @@
                 put(blk(0, rels[xi]), zp(xi, 1), up)
                 put(blk(0, rels[xi]), zm(xi, 1), down)
 
-            put(blk(0, 0), 0, right)
-            put(blk(0, 0), 1, left)
-            z_out(0)
+            places = [(0, right), (1, left), (zp(0, 1), up), (zm(0, 1), down)]
+            put_own(own_row, places)
+            own_copy().wait_recv()
+            put_own(other_row, places)
             filler()
             got(blk(0, -1), 0)
             put(blk(0, -1, lo), 2, right)
@@ -260,24 +267,23 @@
                 flip_other(i)
         for _ in range(MICRO):
             filler()
+
+    own_copy().start()
+    cols_a, cols_b = pl.ds(0, CA), pl.ds(CA, D - CA)
+
+    @pl.when(c == 0)
+    def _():
+        gather("z", cols_a, cols_b, None)
+
+    @pl.when(c == 1)
+    def _():
+        gather("x", cols_b, cols_a, None)
+
+    def gathered(cols):
         everything = wg.at[pl.ds(0, NC - 1), :, cols]
         remote(everything, everything, ag_s.at[0], ag_r.at[0], partner).wait_send()
         remote(everything, everything, d_s.at[0], d_r.at[0], partner).wait_send()
 
-    own_copy().start()
-    own_copy().wait_recv()
-    cols_a, cols_b = pl.ds(0, CA), pl.ds(CA, D - CA)
-
-    @pl.when(c == 0)
-    def _():
-        gather("z", cols_a, cols_b, None)
-
-    @pl.when(c == 1)
-    def _():
-        gather("x", cols_b, cols_a, None)
-
-    own_copy().wait_send()
-
     @pl.when(s == S - 1)
     def _():
         load_cot().wait()
@@ -294,8 +300,8 @@
     def place(u, base=0):
         return u // H, pl.ds(pl.multiple_of(base + (u % H) * R, R), R)
 
-    def differentiate(u):
-        m, rows = place(u)
+    def differentiate(m, rows):
+        R = rows.size
         g = gs[m, rows, :]
         inv = invs[m, rows, 0:1]
         dots = jnp.zeros((R, 1), jnp.float32)
@@ -306,12 +312,12 @@
             both = branch * whitened
             gacc[:, cols] += jnp.sum(both.reshape(R // 8, 8, QW), axis=0)
             dots = dots + jnp.sum(both * gain_ref[:, cols], axis=-1, keepdims=True)
-            gained[:, cols] = branch * gain_ref[:, cols]
+            gained[pl.ds(0, R), cols] = branch * gain_ref[:, cols]
         mean = dots / D
         for q in range(NQ):
             cols = pl.ds(q * QW, QW)
             whitened = xs[m, rows, cols].astype(jnp.float32) * inv
-            fresh = gs[m, rows, cols].astype(jnp.float32) + inv * (gained[:, cols] - whitened * mean)
+            fresh = gs[m, rows, cols].astype(jnp.float32) + inv * (gained[pl.ds(0, R), cols] - whitened * mean)
             outs[m, rows, cols] = fresh.astype(jnp.bfloat16)
 
     quarter = NC * SR // H
@@ -338,9 +344,9 @@
 
         share(m, rows, place(u, TR)[1]).start()
 
-        @pl.when(u >= lag)
+        @pl.when(u > lag)
         def _():
-            differentiate(u - lag)
+            differentiate(*place(u - lag))
 
         @pl.when(s > 0)
         def _():
@@ -356,14 +362,28 @@
 
         return carry
 
-    lax.fori_loop(0, U, tick, 0)
+    for k in range(2):
+        rows, there = pl.ds(k * (R // 2), R // 2), pl.ds(TR + k * (R // 2), R // 2)
+        sem = U if k else 0
+
+        @pl.when(s < S - 1)
+        def _():
+            hand_down(0, rows, sem).wait_recv()
+
+        share(0, rows, there).start()
+        differentiate(0, rows)
+
+        @pl.when(s > 0)
+        def _():
+            hand_down(0, rows, sem).start()
+
+    lax.fori_loop(1, U, tick, 0)
     meet(MICRO - 1)
 
-    def last(r, carry):
-        weigh(MICRO - 1, r)
-        return carry
-
-    lax.fori_loop(0, H, last, 0)
+    far_part = (((z + NZP) % Z) * H) // Z
+
+    def final(k):
+        weigh(MICRO - 1, (far_part + k + H) % H)
 
     def spread(src, dst, place, targets, ss, rs, sem0):
         return [remote(src, dst.at[place], ss.at[sem0 + k], rs.at[sem0 + k], t) for k, t in enumerate(targets)]
@@ -385,7 +405,7 @@
     def hook_a():
         @pl.when(s == 0)
         def _():
-            differentiate(U - 1)
+            differentiate(*place(U - 1))
 
         save().start()
         gv[0] = jnp.sum(gacc[...], axis=0, keepdims=True)
@@ -471,9 +491,14 @@
                         value = value + taken(zslot + NZP)
                     wgf[...] = value
 
+            final(0)
+            final(1)
             for i in range(Z + 4):
                 if i < Z:
                     one(i)
+                if i == 1:
+                    final(-1)
+                    final(2)
                 if 0 <= i - 2 < Z:
                     two(i - 2)
                 if 0 <= i - 4 < Z:
@@ -509,7 +534,11 @@
                     value = value + taken(base + most_p)
                 return value
 
+            for k in (0, 1, -1):
+                final(k)
             for t in range(NZP):
+                if t == 1:
+                    final(2)
                 for xi in range(4):
                     most_p, most_m = hops[xi]
                     base = xi * (Z - 1)
@@ -554,9 +583,27 @@
     row_new = DECAY_RATE * row_old + (1.0 - DECAY_RATE) * (row_sum / D)
     rown_ref[...] = jnp.sum(jnp.where(eye, jnp.broadcast_to(row_new, (SR, SR)), 0.0), axis=0, keepdims=True)
     per_row = 1.0 / row_new
-    tv[0, :, pl.ds(0, D)] = jnp.sum(grad * grad + SQUARE_EPS, axis=0, keepdims=True)
-    tv[0, :, pl.ds(D, D)] = jnp.sum(grad * grad * per_row, axis=0, keepdims=True)
-    tv[0, :, pl.ds(2 * D, 128)] = jnp.broadcast_to(jnp.sum(row_new, axis=0, keepdims=True), (1, 128))
+    E = 2 * X
+    SL = D // E
+    e = x * 2 + c
+    col_sum = jnp.sum(grad * grad + SQUARE_EPS, axis=0, keepdims=True)
+    col_part = jnp.sum(grad * grad * per_row, axis=0, keepdims=True)
+    row_total = jnp.broadcast_to(jnp.sum(row_new, axis=0, keepdims=True), (1, 128))
+    for k in range(E):
+        cols = slice(k * SL, (k + 1) * SL)
+        tv[k, :, pl.ds(0, SL)] = col_sum[:, cols]
+        tv[k, :, pl.ds(SL, SL)] = col_part[:, cols]
+        tv[k, :, pl.ds(2 * SL, 128)] = row_total
+
+    def slice_of(k):
+        return ((x + k // 2) % X) * 2 + (c + k) % 2
+
+    first = [
+        remote(tv.at[slice_of(k)], t1.at[e], t_s.at[k - 1], t_r.at[k - 1], p)
+        for k, p in enumerate(near, start=1)
+    ]
+    second = spread(tu, t2, z, far, t_s, t_r, E - 1)
+    third = spread(tw, t3, e, near, t_s, t_r, E + Z - 2)
 
     def exchange(copies, dst, place, value):
         for copy in copies:
@@ -566,21 +613,36 @@
             copy.wait_recv()
         return added(dst)
 
-    near_copies = spread(tv.at[0], t1, x * 2 + c, near, t_s, t_r, 0)
-    far_copies = spread(tv.at[1], t2, z, far, t_s, t_r, 2 * X - 1)
-    tv[1] = exchange(near_copies, t1, x * 2 + c, tv[0])
-    sums = exchange(far_copies, t2, z, tv[1])
-    col_new = DECAY_RATE * col_ref[...] + (1.0 - DECAY_RATE) * sums[:, 0:D] / D
-    coln_ref[...] = col_new
-    row_mean = sums[:, 2 * D : 2 * D + 1] / D
-    total_square = row_mean * jnp.sum(sums[:, D : 2 * D] / col_new, axis=-1, keepdims=True)
+    tu[...] = exchange(first, t1, e, tv[e])
+    sums = exchange(second, t2, z, tu[...])
+    col_old = col_ref[:, pl.ds(pl.multiple_of(e * SL, SL), SL)]
+    fresh_cols = DECAY_RATE * col_old + (1.0 - DECAY_RATE) * sums[:, 0:SL] / D
+    tw[:, pl.ds(0, SL)] = fresh_cols
+    share_sum = jnp.sum(sums[:, SL : 2 * SL] / fresh_cols, axis=-1, keepdims=True)
+    tw[:, pl.ds(SL, 128)] = jnp.broadcast_to(share_sum, (1, 128))
+    shares = exchange(third, t3, e, tw[...])
+    for k in range(E):
+        coln_ref[:, pl.ds(k * SL, SL)] = t3[k, :, pl.ds(0, SL)]
+    col_new = coln_ref[...]
+    row_mean = sums[:, 2 * SL : 2 * SL + 1] / D
+    total_square = row_mean * shares[:, SL : SL + 1]
     clip = jnp.maximum(1.0, jnp.sqrt(total_square / (D * D)))
     step_ref[...] = grad / jnp.sqrt(row_new * col_new / row_mean) / clip
     for copy in gain_far():
         copy.wait_recv()
     gg_ref[...] = added(g2)
 
-    for copy in near_copies + far_copies + gain_near() + gain_far():
+    own_copy().wait_send()
+
+    @pl.when(c == 0)
+    def _():
+        gathered(cols_a)
+
+    @pl.when(c == 1)
+    def _():
+        gathered(cols_b)
+
+    for copy in first + second + third + gain_near() + gain_far():
         copy.wait_send()
     save().wait()
     for m in range(MICRO):
@@ -626,6 +688,7 @@
     R = TR // 4
     CA = D * 9 // 16
     U = MICRO * (TR // R)
+    SL = D // (2 * X)
     bf, f32 = jnp.bfloat16, jnp.float32
     dma = pltpu.SemaphoreType.DMA
     vmem = pl.BlockSpec(memory_space=pltpu.VMEM)
@@ -646,9 +709,12 @@
         V((SR, D), f32),
         V((NC - 1, SR, D), bf),
         V((NC - 1, SR, D), bf),
-        V((2, 1, 2 * D + 128), f32),
-        V((2 * X, 1, 2 * D + 128), f32),
-        V((Z, 1, 2 * D + 128), f32),
+        V((2 * X, 1, 2 * SL + 128), f32),
+        V((2 * X, 1, 2 * SL + 128), f32),
+        V((1, 2 * SL + 128), f32),
+        V((Z, 1, 2 * SL + 128), f32),
+        V((1, SL + 128), f32),
+        V((2 * X, 1, SL + 128), f32),
         V((2, 1, D), f32),
         V((2 * X, 1, D), f32),
         V((Z, 1, D), f32),
@@ -664,13 +730,13 @@
         dma((MICRO,)),
         dma((MICRO,)),
         dma((1,)),
-        dma((U,)),
+        dma((U + 1,)),
         dma((1,)),
         dma((MICRO,)),
         dma((1,)),
         dma((5 * Z,)),
-        dma((2 * X + Z,)),
-        dma((2 * X + Z,)),
+        dma((4 * X + Z,)),
+        dma((4 * X + Z,)),
         dma((2 * X + Z,)),
         dma((2 * X + Z,)),
     ]

time: 156 us -> 156 us (level)
  no operation moved by 1% of the time
where the time goes in v4:
time: 156 us; the launch traced here: 155 us
  Pallas kernels  155 us (99%)
    pallas_call x1, Pallas kernels, body(): pl.pallas_call(functools.partial(kernel, S, Z, R, CA), out_shape=(jax.Sha...  152 us

profile of v4, /device:TPU:1, one launch (start us, length us, event | category | flops | bytes accessed | tf_op | source)
XLA Modules:
  0.0 155.4 jit_solution(6404269316709253310)
XLA Ops:
  0.6 152.0 %relay_back.1 = (bf16[4,128,2048]{2,1,0:T(8,128)(2,1)}, f32[32,2048]{1,0:T(8,128)}, f32[1,32]{1,0:T(1,128)}, f32[1,2048]{1,0:T(1,128)}, f32[1,2048]{1,0:T(1,128)}) custom-call(bf16[4,128,2048]{2,1,0:T(8,128)(2,1)} %bitcast.4, bf16[4,128,2048]{2,1,0:T(8,128)(2,1)} %cot_hbm.1, bf16[32,2048]{1,0:T(8,128)(2,1)} %bitcast.5, f32[1,2048]{1,0:T(1,128)} %gain_ref.1, ...), custom_call_target="tpu_custom_call" | custom-call | tf_op jit(solution)/shard_map/relay_back/pallas_call | solution.py:743
  152.7 2.6 %deliver.1 = (bf16[4,128,2048]{2,1,0:T(8,128)(2,1)}, f32[32,2048]{1,0:T(8,128)}, f32[1,32]{1,0:T(1,128)}, f32[1,2048]{1,0:T(1,128)}, f32[1,2048]{1,0:T(1,128)}) custom-call(bf16[4,128,2048]{2,1,0:T(8,128)(2,1)} %get-tuple-element.15.refs_0_, f32[32,2048]{1,0:T(8,128)} %get-tuple-element.16.refs_1_, f32[1,32]{1,0:T(1,128)} %get-tuple-element.17.refs_2_, ...), custom_call_target="tpu_custom_call" | custom-call | tf_op jit(solution)/shard_map/deliver/pallas_call | solution.py:760

commit v5 on v4

--- a/solution.py
+++ b/solution.py
@@ -20,7 +20,7 @@
     S, Z, R, CA,
     x_hbm, cot_hbm, w_ref, gain_ref, row_ref, col_ref,
     out_hbm, step_ref, rown_ref, coln_ref, gg_ref,
-    xs, gs, outs, wg, wt, nt, lt, acc, gained, invs, gacc, wgf, rbuf, sbuf, tv, t1, tu, t2, tw, t3, gv, g1, g2,
+    xs, gs, outs, wg, wt, nt, lt, acc, gained, invs, gacc, wgf, pre, rbuf, sbuf, tv, t1, tu, t2, tw, t3, gv, g1, g2,
     in_sem, lsem, out_sem, ag_s, ag_r, d_s, d_r, own_s, own_r, l_s, l_r,
     y_s, y_r, f_s, f_r, rs_s, rs_r, t_s, t_r, g_s, g_r,
 ):
@@ -133,6 +133,14 @@
             whole = wg.at[pl.ds(0, n), :, other_cols]
             remote(whole, whole, d_s.at[0], d_r.at[i], partner).wait_recv()
             flip(i, other_cols)
+
+            @pl.when(s == S - 1)
+            def _():
+                width = X * 2 * SR
+                ready = pl.ds(pl.multiple_of(((z + group(i) + Z) % Z) * width, width), width)
+                pre[:, ready] = lax.dot_general(
+                    gs[0, pl.ds(0, TR), :], wt[:, ready], NN, preferred_element_type=jnp.float32
+                )
 
         def got(view, sem):
             remote(view, view, ag_s.at[0], ag_r.at[sem], partner).wait_recv()
@@ -269,6 +277,11 @@
             filler()
 
     own_copy().start()
+
+    @pl.when(s == S - 1)
+    def _():
+        load_cot().wait()
+
     cols_a, cols_b = pl.ds(0, CA), pl.ds(CA, D - CA)
 
     @pl.when(c == 0)
@@ -284,10 +297,6 @@
         remote(everything, everything, ag_s.at[0], ag_r.at[0], partner).wait_send()
         remote(everything, everything, d_s.at[0], d_r.at[0], partner).wait_send()
 
-    @pl.when(s == S - 1)
-    def _():
-        load_cot().wait()
-
     def hand_down(m, rows, u):
         return remote(outs.at[m, rows], gs.at[m, rows], y_s.at[0], y_r.at[u], (s - 1, dp))
 
@@ -300,14 +309,17 @@
     def place(u, base=0):
         return u // H, pl.ds(pl.multiple_of(base + (u % H) * R, R), R)
 
-    def differentiate(m, rows):
+    def differentiate(m, rows, ready=False):
         R = rows.size
         g = gs[m, rows, :]
         inv = invs[m, rows, 0:1]
         dots = jnp.zeros((R, 1), jnp.float32)
         for q in range(NQ):
             cols = pl.ds(q * QW, QW)
-            branch = lax.dot_general(g, wt[:, cols], NN, preferred_element_type=jnp.float32)
+            if ready:
+                branch = pre[rows, cols]
+            else:
+                branch = lax.dot_general(g, wt[:, cols], NN, preferred_element_type=jnp.float32)
             whitened = xs[m, rows, cols].astype(jnp.float32) * inv
             both = branch * whitened
             gacc[:, cols] += jnp.sum(both.reshape(R // 8, 8, QW), axis=0)
@@ -342,15 +354,21 @@
         def _():
             hand_down(m, rows, u).wait_recv()
 
-        share(m, rows, place(u, TR)[1]).start()
-
-        @pl.when(u > lag)
+        early = jnp.logical_and(s == S - 1, u < H)
+
+        @pl.when(jnp.logical_and(u > lag, jnp.logical_not(early)))
         def _():
             differentiate(*place(u - lag))
+
+        @pl.when(early)
+        def _():
+            differentiate(m, rows, True)
 
         @pl.when(s > 0)
         def _():
             hand_down(m, rows, u).start()
+
+        share(m, rows, place(u, TR)[1]).start()
 
         @pl.when(u >= H)
         def _():
@@ -369,13 +387,17 @@
         @pl.when(s < S - 1)
         def _():
             hand_down(0, rows, sem).wait_recv()
-
-        share(0, rows, there).start()
-        differentiate(0, rows)
+            differentiate(0, rows)
+
+        @pl.when(s == S - 1)
+        def _():
+            differentiate(0, rows, True)
 
         @pl.when(s > 0)
         def _():
             hand_down(0, rows, sem).start()
+
+        share(0, rows, there).start()
 
     lax.fori_loop(1, U, tick, 0)
     meet(MICRO - 1)
@@ -583,6 +605,7 @@
     row_new = DECAY_RATE * row_old + (1.0 - DECAY_RATE) * (row_sum / D)
     rown_ref[...] = jnp.sum(jnp.where(eye, jnp.broadcast_to(row_new, (SR, SR)), 0.0), axis=0, keepdims=True)
     per_row = 1.0 / row_new
+    wgf[...] = grad * lax.rsqrt(row_new)
     E = 2 * X
     SL = D // E
     e = x * 2 + c
@@ -627,7 +650,7 @@
     row_mean = sums[:, 2 * SL : 2 * SL + 1] / D
     total_square = row_mean * shares[:, SL : SL + 1]
     clip = jnp.maximum(1.0, jnp.sqrt(total_square / (D * D)))
-    step_ref[...] = grad / jnp.sqrt(row_new * col_new / row_mean) / clip
+    step_ref[...] = wgf[...] * (lax.rsqrt(col_new) * (jnp.sqrt(row_mean) / clip))
     for copy in gain_far():
         copy.wait_recv()
     gg_ref[...] = added(g2)
@@ -662,14 +685,18 @@
     for src, mid, dst in zip(sources, held, results):
         pieces = src.shape[0] if len(src.shape) == 3 else 1
         for k in range(pieces):
-            a, m, b = (src.at[k], mid.at[k], dst.at[k]) if pieces > 1 else (src, mid, dst)
-            i = len(ways)
-            ways.append(
-                (
-                    pltpu.make_async_copy(a, m, sems.at[0, i]),
-                    pltpu.make_async_copy(m, b, sems.at[1, i]),
+            trio = (src.at[k], mid.at[k], dst.at[k]) if pieces > 1 else (src, mid, dst)
+            half = trio[0].shape[0] // 2
+            parts = [pl.ds(0, half), pl.ds(half, half)] if pieces > 1 else [None]
+            for part in parts:
+                a, m, b = trio if part is None else [ref.at[part] for ref in trio]
+                i = len(ways)
+                ways.append(
+                    (
+                        pltpu.make_async_copy(a, m, sems.at[0, i]),
+                        pltpu.make_async_copy(m, b, sems.at[1, i]),
+                    )
                 )
-            )
     for into, _ in ways:
         into.start()
     for into, out in ways:
@@ -707,6 +734,7 @@
         V((MICRO, TR, 128), f32),
         V((8, D), f32),
         V((SR, D), f32),
+        V((TR, D), f32),
         V((NC - 1, SR, D), bf),
         V((NC - 1, SR, D), bf),
         V((2 * X, 1, 2 * SL + 128), f32),
@@ -762,7 +790,7 @@
         out_shape=tuple(jax.ShapeDtypeStruct(o.shape, o.dtype) for o in outs),
         in_specs=[hbm] * 5,
         out_specs=(hbm,) * 5,
-        scratch_shapes=[V(o.shape, o.dtype) for o in outs] + [dma((2, MICRO + 4))],
+        scratch_shapes=[V(o.shape, o.dtype) for o in outs] + [dma((2, 2 * MICRO + 4))],
         name="deliver",
     )(*outs)
     return (outs[0][None], outs[1][None], outs[2], outs[3], outs[4])

time: 156 us -> 158 us (1.013)
  Pallas kernels: 155 us -> 157 us
    pallas_call x1, Pallas kernels: 152 us -> 154 us  [body(): pl.pallas_call(functools.partial(kernel, S, Z, R, CA), out_shape=(jax.Sha...]
where the time goes in v5:
time: 158 us
  Pallas kernels  157 us (99%)
    pallas_call x1, Pallas kernels, body(): pl.pallas_call(functools.partial(kernel, S, Z, R, CA), out_shape=(jax.Sha...  154 us

profile of v5, /device:TPU:1, one launch (start us, length us, event | category | flops | bytes accessed | tf_op | source)
XLA Modules:
  0.0 157.6 jit_solution(11742603721972763306)
XLA Ops:
  0.6 154.2 %relay_back.1 = (bf16[4,128,2048]{2,1,0:T(8,128)(2,1)}, f32[32,2048]{1,0:T(8,128)}, f32[1,32]{1,0:T(1,128)}, f32[1,2048]{1,0:T(1,128)}, f32[1,2048]{1,0:T(1,128)}) custom-call(bf16[4,128,2048]{2,1,0:T(8,128)(2,1)} %bitcast.4, bf16[4,128,2048]{2,1,0:T(8,128)(2,1)} %cot_hbm.1, bf16[32,2048]{1,0:T(8,128)(2,1)} %bitcast.5, f32[1,2048]{1,0:T(1,128)} %gain_ref.1, ...), custom_call_target="tpu_custom_call" | custom-call | tf_op jit(solution)/shard_map/relay_back/pallas_call | solution.py:771
  154.9 2.6 %deliver.1 = (bf16[4,128,2048]{2,1,0:T(8,128)(2,1)}, f32[32,2048]{1,0:T(8,128)}, f32[1,32]{1,0:T(1,128)}, f32[1,2048]{1,0:T(1,128)}, f32[1,2048]{1,0:T(1,128)}) custom-call(bf16[4,128,2048]{2,1,0:T(8,128)(2,1)} %get-tuple-element.15.refs_0_, f32[32,2048]{1,0:T(8,128)} %get-tuple-element.16.refs_1_, f32[1,32]{1,0:T(1,128)} %get-tuple-element.17.refs_2_, ...), custom_call_target="tpu_custom_call" | custom-call | tf_op jit(solution)/shard_map/deliver/pallas_call | solution.py:788

commit v6 on v5

--- a/solution.py
+++ b/solution.py
@@ -20,7 +20,7 @@
     S, Z, R, CA,
     x_hbm, cot_hbm, w_ref, gain_ref, row_ref, col_ref,
     out_hbm, step_ref, rown_ref, coln_ref, gg_ref,
-    xs, gs, outs, wg, wt, nt, lt, acc, gained, invs, gacc, wgf, pre, rbuf, sbuf, tv, t1, tu, t2, tw, t3, gv, g1, g2,
+    xs, gs, outs, wg, wt, nt, lt, acc, gained, invs, gacc, wgf, rbuf, sbuf, tv, t1, tu, t2, tw, t3, gv, g1, g2,
     in_sem, lsem, out_sem, ag_s, ag_r, d_s, d_r, own_s, own_r, l_s, l_r,
     y_s, y_r, f_s, f_r, rs_s, rs_r, t_s, t_r, g_s, g_r,
 ):
@@ -133,14 +133,6 @@
             whole = wg.at[pl.ds(0, n), :, other_cols]
             remote(whole, whole, d_s.at[0], d_r.at[i], partner).wait_recv()
             flip(i, other_cols)
-
-            @pl.when(s == S - 1)
-            def _():
-                width = X * 2 * SR
-                ready = pl.ds(pl.multiple_of(((z + group(i) + Z) % Z) * width, width), width)
-                pre[:, ready] = lax.dot_general(
-                    gs[0, pl.ds(0, TR), :], wt[:, ready], NN, preferred_element_type=jnp.float32
-                )
 
         def got(view, sem):
             remote(view, view, ag_s.at[0], ag_r.at[sem], partner).wait_recv()
@@ -214,12 +206,11 @@
                 x_mid(*pair)
             for pair in ends:
                 x_end(*pair)
-            for i in range(Z - 3):
+            for i in range(Z - 1):
                 flip_other(i)
             for pair in mids:
                 x_end(*pair)
-            for i in range(Z - 3, Z):
-                flip_other(i)
+            flip_other(Z - 1)
         else:
             rels = [0, -1, 1, 2]
             hops = [(NZP, NZM), (NZM, NZP), (NZP, NZM), (NZM, NZP)]
@@ -309,17 +300,14 @@
     def place(u, base=0):
         return u // H, pl.ds(pl.multiple_of(base + (u % H) * R, R), R)
 
-    def differentiate(m, rows, ready=False):
+    def differentiate(m, rows):
         R = rows.size
         g = gs[m, rows, :]
         inv = invs[m, rows, 0:1]
         dots = jnp.zeros((R, 1), jnp.float32)
         for q in range(NQ):
             cols = pl.ds(q * QW, QW)
-            if ready:
-                branch = pre[rows, cols]
-            else:
-                branch = lax.dot_general(g, wt[:, cols], NN, preferred_element_type=jnp.float32)
+            branch = lax.dot_general(g, wt[:, cols], NN, preferred_element_type=jnp.float32)
             whitened = xs[m, rows, cols].astype(jnp.float32) * inv
             both = branch * whitened
             gacc[:, cols] += jnp.sum(both.reshape(R // 8, 8, QW), axis=0)
@@ -354,15 +342,9 @@
         def _():
             hand_down(m, rows, u).wait_recv()
 
-        early = jnp.logical_and(s == S - 1, u < H)
-
-        @pl.when(jnp.logical_and(u > lag, jnp.logical_not(early)))
+        @pl.when(u > lag)
         def _():
             differentiate(*place(u - lag))
-
-        @pl.when(early)
-        def _():
-            differentiate(m, rows, True)
 
         @pl.when(s > 0)
         def _():
@@ -387,11 +369,8 @@
         @pl.when(s < S - 1)
         def _():
             hand_down(0, rows, sem).wait_recv()
-            differentiate(0, rows)
-
-        @pl.when(s == S - 1)
-        def _():
-            differentiate(0, rows, True)
+
+        differentiate(0, rows)
 
         @pl.when(s > 0)
         def _():
@@ -734,7 +713,6 @@
         V((MICRO, TR, 128), f32),
         V((8, D), f32),
         V((SR, D), f32),
-        V((TR, D), f32),
         V((NC - 1, SR, D), bf),
         V((NC - 1, SR, D), bf),
         V((2 * X, 1, 2 * SL + 128), f32),

time: 158 us -> 159 us (level)
  no operation moved by 1% of the time
where the time goes in v6:
time: 159 us; the launch traced here: 158 us
  Pallas kernels  158 us (99%)
    pallas_call x1, Pallas kernels, body(): pl.pallas_call(functools.partial(kernel, S, Z, R, CA), out_shape=(jax.Sha...  155 us

profile of v6, /device:TPU:1, one launch (start us, length us, event | category | flops | bytes accessed | tf_op | source)
XLA Modules:
  0.0 158.4 jit_solution(14784006057604728057)
XLA Ops:
  0.6 155.0 %relay_back.1 = (bf16[4,128,2048]{2,1,0:T(8,128)(2,1)}, f32[32,2048]{1,0:T(8,128)}, f32[1,32]{1,0:T(1,128)}, f32[1,2048]{1,0:T(1,128)}, f32[1,2048]{1,0:T(1,128)}) custom-call(bf16[4,128,2048]{2,1,0:T(8,128)(2,1)} %bitcast.4, bf16[4,128,2048]{2,1,0:T(8,128)(2,1)} %cot_hbm.1, bf16[32,2048]{1,0:T(8,128)(2,1)} %bitcast.5, f32[1,2048]{1,0:T(1,128)} %gain_ref.1, ...), custom_call_target="tpu_custom_call" | custom-call | tf_op jit(solution)/shard_map/relay_back/pallas_call | solution.py:749
  155.7 2.6 %deliver.1 = (bf16[4,128,2048]{2,1,0:T(8,128)(2,1)}, f32[32,2048]{1,0:T(8,128)}, f32[1,32]{1,0:T(1,128)}, f32[1,2048]{1,0:T(1,128)}, f32[1,2048]{1,0:T(1,128)}) custom-call(bf16[4,128,2048]{2,1,0:T(8,128)(2,1)} %get-tuple-element.15.refs_0_, f32[32,2048]{1,0:T(8,128)} %get-tuple-element.16.refs_1_, f32[1,32]{1,0:T(1,128)} %get-tuple-element.17.refs_2_, ...), custom_call_target="tpu_custom_call" | custom-call | tf_op jit(solution)/shard_map/deliver/pallas_call | solution.py:766

commit v7 on v6

--- a/solution.py
+++ b/solution.py
@@ -20,7 +20,7 @@
     S, Z, R, CA,
     x_hbm, cot_hbm, w_ref, gain_ref, row_ref, col_ref,
     out_hbm, step_ref, rown_ref, coln_ref, gg_ref,
-    xs, gs, outs, wg, wt, nt, lt, acc, gained, invs, gacc, wgf, rbuf, sbuf, tv, t1, tu, t2, tw, t3, gv, g1, g2,
+    xs, gs, outs, wg, wt, nt, lt, acc, gained, invs, gacc, wgf, rbuf, sbuf, tv, t1, t2, gv, g1, g2,
     in_sem, lsem, out_sem, ag_s, ag_r, d_s, d_r, own_s, own_r, l_s, l_r,
     y_s, y_r, f_s, f_r, rs_s, rs_r, t_s, t_r, g_s, g_r,
 ):
@@ -342,6 +342,8 @@
         def _():
             hand_down(m, rows, u).wait_recv()
 
+        share(m, rows, place(u, TR)[1]).start()
+
         @pl.when(u > lag)
         def _():
             differentiate(*place(u - lag))
@@ -349,8 +351,6 @@
         @pl.when(s > 0)
         def _():
             hand_down(m, rows, u).start()
-
-        share(m, rows, place(u, TR)[1]).start()
 
         @pl.when(u >= H)
         def _():
@@ -370,13 +370,12 @@
         def _():
             hand_down(0, rows, sem).wait_recv()
 
+        share(0, rows, there).start()
         differentiate(0, rows)
 
         @pl.when(s > 0)
         def _():
             hand_down(0, rows, sem).start()
-
-        share(0, rows, there).start()
 
     lax.fori_loop(1, U, tick, 0)
     meet(MICRO - 1)
@@ -585,27 +584,9 @@
     rown_ref[...] = jnp.sum(jnp.where(eye, jnp.broadcast_to(row_new, (SR, SR)), 0.0), axis=0, keepdims=True)
     per_row = 1.0 / row_new
     wgf[...] = grad * lax.rsqrt(row_new)
-    E = 2 * X
-    SL = D // E
-    e = x * 2 + c
-    col_sum = jnp.sum(grad * grad + SQUARE_EPS, axis=0, keepdims=True)
-    col_part = jnp.sum(grad * grad * per_row, axis=0, keepdims=True)
-    row_total = jnp.broadcast_to(jnp.sum(row_new, axis=0, keepdims=True), (1, 128))
-    for k in range(E):
-        cols = slice(k * SL, (k + 1) * SL)
-        tv[k, :, pl.ds(0, SL)] = col_sum[:, cols]
-        tv[k, :, pl.ds(SL, SL)] = col_part[:, cols]
-        tv[k, :, pl.ds(2 * SL, 128)] = row_total
-
-    def slice_of(k):
-        return ((x + k // 2) % X) * 2 + (c + k) % 2
-
-    first = [
-        remote(tv.at[slice_of(k)], t1.at[e], t_s.at[k - 1], t_r.at[k - 1], p)
-        for k, p in enumerate(near, start=1)
-    ]
-    second = spread(tu, t2, z, far, t_s, t_r, E - 1)
-    third = spread(tw, t3, e, near, t_s, t_r, E + Z - 2)
+    tv[0, :, pl.ds(0, D)] = jnp.sum(grad * grad + SQUARE_EPS, axis=0, keepdims=True)
+    tv[0, :, pl.ds(D, D)] = jnp.sum(grad * grad * per_row, axis=0, keepdims=True)
+    tv[0, :, pl.ds(2 * D, 128)] = jnp.broadcast_to(jnp.sum(row_new, axis=0, keepdims=True), (1, 128))
 
     def exchange(copies, dst, place, value):
         for copy in copies:
@@ -615,19 +596,14 @@
             copy.wait_recv()
         return added(dst)
 
-    tu[...] = exchange(first, t1, e, tv[e])
-    sums = exchange(second, t2, z, tu[...])
-    col_old = col_ref[:, pl.ds(pl.multiple_of(e * SL, SL), SL)]
-    fresh_cols = DECAY_RATE * col_old + (1.0 - DECAY_RATE) * sums[:, 0:SL] / D
-    tw[:, pl.ds(0, SL)] = fresh_cols
-    share_sum = jnp.sum(sums[:, SL : 2 * SL] / fresh_cols, axis=-1, keepdims=True)
-    tw[:, pl.ds(SL, 128)] = jnp.broadcast_to(share_sum, (1, 128))
-    shares = exchange(third, t3, e, tw[...])
-    for k in range(E):
-        coln_ref[:, pl.ds(k * SL, SL)] = t3[k, :, pl.ds(0, SL)]
-    col_new = coln_ref[...]
-    row_mean = sums[:, 2 * SL : 2 * SL + 1] / D
-    total_square = row_mean * shares[:, SL : SL + 1]
+    first = spread(tv.at[0], t1, x * 2 + c, near, t_s, t_r, 0)
+    second = spread(tv.at[1], t2, z, far, t_s, t_r, 2 * X - 1)
+    tv[1] = exchange(first, t1, x * 2 + c, tv[0])
+    sums = exchange(second, t2, z, tv[1])
+    col_new = DECAY_RATE * col_ref[...] + (1.0 - DECAY_RATE) * sums[:, 0:D] / D
+    coln_ref[...] = col_new
+    row_mean = sums[:, 2 * D : 2 * D + 1] / D
+    total_square = row_mean * jnp.sum(sums[:, D : 2 * D] / col_new, axis=-1, keepdims=True)
     clip = jnp.maximum(1.0, jnp.sqrt(total_square / (D * D)))
     step_ref[...] = wgf[...] * (lax.rsqrt(col_new) * (jnp.sqrt(row_mean) / clip))
     for copy in gain_far():
@@ -644,7 +620,7 @@
     def _():
         gathered(cols_b)
 
-    for copy in first + second + third + gain_near() + gain_far():
+    for copy in first + second + gain_near() + gain_far():
         copy.wait_send()
     save().wait()
     for m in range(MICRO):
@@ -694,7 +670,6 @@
     R = TR // 4
     CA = D * 9 // 16
     U = MICRO * (TR // R)
-    SL = D // (2 * X)
     bf, f32 = jnp.bfloat16, jnp.float32
     dma = pltpu.SemaphoreType.DMA
     vmem = pl.BlockSpec(memory_space=pltpu.VMEM)
@@ -715,12 +690,9 @@
         V((SR, D), f32),
         V((NC - 1, SR, D), bf),
         V((NC - 1, SR, D), bf),
-        V((2 * X, 1, 2 * SL + 128), f32),
-        V((2 * X, 1, 2 * SL + 128), f32),
-        V((1, 2 * SL + 128), f32),
-        V((Z, 1, 2 * SL + 128), f32),
-        V((1, SL + 128), f32),
-        V((2 * X, 1, SL + 128), f32),
+        V((2, 1, 2 * D + 128), f32),
+        V((2 * X, 1, 2 * D + 128), f32),
+        V((Z, 1, 2 * D + 128), f32),
         V((2, 1, D), f32),
         V((2 * X, 1, D), f32),
         V((Z, 1, D), f32),
@@ -741,8 +713,8 @@
         dma((MICRO,)),
         dma((1,)),
         dma((5 * Z,)),
-        dma((4 * X + Z,)),
-        dma((4 * X + Z,)),
+        dma((2 * X + Z,)),
+        dma((2 * X + Z,)),
         dma((2 * X + Z,)),
         dma((2 * X + Z,)),
     ]

time: 159 us -> 154 us (0.969)
  Pallas kernels: 158 us -> 152 us
    pallas_call x1, Pallas kernels: 155 us -> 150 us  [body(): pl.pallas_call(functools.partial(kernel, S, Z, R, CA), out_shape=(jax.Sha...]
where the time goes in v7:
time: 154 us; the launch traced here: 153 us
  Pallas kernels  152 us (99%)
    pallas_call x1, Pallas kernels, body(): pl.pallas_call(functools.partial(kernel, S, Z, R, CA), out_shape=(jax.Sha...  150 us

profile of v7, /device:TPU:1, one launch (start us, length us, event | category | flops | bytes accessed | tf_op | source)
XLA Modules:
  0.0 153.1 jit_solution(16917195535718846733)
XLA Ops:
  0.6 149.7 %relay_back.1 = (bf16[4,128,2048]{2,1,0:T(8,128)(2,1)}, f32[32,2048]{1,0:T(8,128)}, f32[1,32]{1,0:T(1,128)}, f32[1,2048]{1,0:T(1,128)}, f32[1,2048]{1,0:T(1,128)}) custom-call(bf16[4,128,2048]{2,1,0:T(8,128)(2,1)} %bitcast.4, bf16[4,128,2048]{2,1,0:T(8,128)(2,1)} %cot_hbm.1, bf16[32,2048]{1,0:T(8,128)(2,1)} %bitcast.5, f32[1,2048]{1,0:T(1,128)} %gain_ref.1, ...), custom_call_target="tpu_custom_call" | custom-call | tf_op jit(solution)/shard_map/relay_back/pallas_call | solution.py:721
  150.4 2.6 %deliver.1 = (bf16[4,128,2048]{2,1,0:T(8,128)(2,1)}, f32[32,2048]{1,0:T(8,128)}, f32[1,32]{1,0:T(1,128)}, f32[1,2048]{1,0:T(1,128)}, f32[1,2048]{1,0:T(1,128)}) custom-call(bf16[4,128,2048]{2,1,0:T(8,128)(2,1)} %get-tuple-element.15.refs_0_, f32[32,2048]{1,0:T(8,128)} %get-tuple-element.16.refs_1_, f32[1,32]{1,0:T(1,128)} %get-tuple-element.17.refs_2_, ...), custom_call_target="tpu_custom_call" | custom-call | tf_op jit(solution)/shard_map/deliver/pallas_call | solution.py:738
